TPU v7x, 1024 devices: a whole 4x8x16 slice. The times are simulated.
1024 devices in a mesh: gx: 4 (over z_hi), gy: 8 (over z_lo, core), gz: 32 (over x, y).
Axes of the slice: x: 4, y: 8, z: 16 (z_hi: 4, z_lo: 4; z = z_hi * 4 + z_lo), core: 2. Of those that a mesh axis runs over, the one named last changes fastest.
Arguments:
- orbitals: float32 [4, 128, 64, 512], P(None, 'gz', 'gy', 'gx'), may hold values from -18 to 18
- potential: float32 [128, 64, 512], P('gz', 'gy', 'gx'), may hold values from -6 to 6
- block_atom: int32 [32, 8, 4, 16], P('gz', 'gy', 'gx'), may hold values from 0 to 3071, as said below
- block_points: int32 [32, 8, 4, 16, 128], P('gz', 'gy', 'gx'), may hold values from 0 to 4095
- block_count: int32 [32, 8, 4], P('gz', 'gy', 'gx'), may hold values from 1 to 16, as said below
- projector_values: float32 [32, 8, 4, 16, 8, 128], P('gz', 'gy', 'gx'), may hold values from -0.5 to 0.5
- coupling: float32 [2, 8, 8], replicated, may hold values from -3 to 3, as said below
Outputs:
- hamiltonian_image: float32 [4, 128, 64, 512], P(None, 'gz', 'gy', 'gx')
- residual: float32 [4, 128, 64, 512], P(None, 'gz', 'gy', 'gx')
Inputs may be any that keep to these rules, and one draw needn't show every extreme that they name: `block_atom`: atoms are numbered by owning box, boxes numbered z slowest, then y, then x: atom a is owned by box a // 3. The owner of a slot's atom lies at most one box away from the slot's box along each of the three directions, the boxes wrapping around. A box's slots from block_count on are padding. `coupling`: Symmetric.
All inputs are finite; a program needn't handle non-finite values.
Results may differ from a plain program's by a relative error of at most 0.00005.
Values sent between devices are 32-bit elements; how exact they have to be, the bound alone decides.
A program may use at most 64 MiB of HBM per device.

v0:
```python
import jax
import jax.numpy as jnp
from jax import lax
from jax.sharding import PartitionSpec as P

ATOM_DEV = 3


STENCIL = (-205.0 / 72.0, 8.0 / 5.0, -1.0 / 5.0, 8.0 / 315.0, -1.0 / 560.0)
HIGH = lax.Precision.HIGHEST


def padded_2(cells, sides, width):
    for axis, dim in sides:
        count = lax.axis_size(axis)
        head = lax.slice_in_dim(cells, 0, width, axis=dim)
        tail = lax.slice_in_dim(cells, cells.shape[dim] - width, cells.shape[dim], axis=dim)
        cells = jnp.concatenate(
            [
                lax.ppermute(tail, axis, [(i, (i + 1) % count) for i in range(count)]),
                cells,
                lax.ppermute(head, axis, [((i + 1) % count, i) for i in range(count)]),
            ],
            axis=dim,
        )
    return cells


def coupling_for(coupling, atom_ids):
    oxygen = (atom_ids % 3 == 0)[:, None, None]
    return jnp.where(oxygen, coupling[0][None], coupling[1][None])


def on_device(
    orbitals, potential, block_atom, block_points, block_count, projector_values, coupling
):
    orbital_count, cells_z, cells_y, cells_x = orbitals.shape
    padded = padded_2(orbitals, (("gx", 3), ("gy", 2), ("gz", 1)), 4)
    kinetic = 3.0 * STENCIL[0] * orbitals
    for offset in range(1, 5):
        weight = STENCIL[offset]
        along_depth = (
            padded[:, 4 + offset : 4 + offset + cells_z, 4 : 4 + cells_y, 4 : 4 + cells_x]
            + padded[:, 4 - offset : 4 - offset + cells_z, 4 : 4 + cells_y, 4 : 4 + cells_x]
        )
        along_rows = (
            padded[:, 4 : 4 + cells_z, 4 + offset : 4 + offset + cells_y, 4 : 4 + cells_x]
            + padded[:, 4 : 4 + cells_z, 4 - offset : 4 - offset + cells_y, 4 : 4 + cells_x]
        )
        along_cols = (
            padded[:, 4 : 4 + cells_z, 4 : 4 + cells_y, 4 + offset : 4 + offset + cells_x]
            + padded[:, 4 : 4 + cells_z, 4 : 4 + cells_y, 4 - offset : 4 - offset + cells_x]
        )
        kinetic = kinetic + weight * (along_depth + along_rows + along_cols)
    kinetic = -0.5 * kinetic
    points_total = cells_z * cells_y * cells_x
    flat_orbitals = orbitals.reshape(orbital_count, points_total)
    atom_ids = block_atom.reshape(-1)
    slot_count = atom_ids.shape[0]
    points = block_points.reshape(slot_count, -1)
    beta_rows = projector_values.reshape(
        slot_count, projector_values.shape[4], projector_values.shape[5]
    )
    projectors = beta_rows.shape[1]
    in_use = (jnp.arange(slot_count, dtype=jnp.int32) < block_count.reshape(())).astype(jnp.float32)
    gathered = flat_orbitals[:, points]
    partial_terms = (
        jnp.einsum("bpq,nbq->bpn", beta_rows, gathered, precision=HIGH) * in_use[:, None, None]
    )
    size_x = lax.axis_size("gx")
    size_y = lax.axis_size("gy")
    size_z = lax.axis_size("gz")
    atom_total = ATOM_DEV * size_x * size_y * size_z
    dense_sums = (
        jnp.zeros((atom_total, projectors, orbital_count), jnp.float32)
        .at[atom_ids]
        .add(partial_terms)
    )
    totals = lax.psum(dense_sums, ("gx", "gy", "gz"))
    applied = jnp.einsum(
        "apq,aqn->apn", coupling_for(coupling, atom_ids), totals[atom_ids], precision=HIGH
    )
    values = jnp.einsum("bpq,bpn->nbq", beta_rows, applied, precision=HIGH) * in_use[None, :, None]
    projected = (
        jnp.zeros((orbital_count, points_total), jnp.float32)
        .at[:, points.reshape(-1)]
        .add(values.reshape(orbital_count, -1))
    )
    image = kinetic + potential[None] * orbitals + projected.reshape(orbitals.shape)
    flat_image = image.reshape(orbital_count, points_total)
    grid_total = points_total * size_x * size_y * size_z
    gram_matrix = (
        lax.psum(jnp.dot(flat_orbitals, flat_image.T, precision=HIGH), ("gx", "gy", "gz"))
        / grid_total
    )
    residual = image - jnp.dot(gram_matrix.T, flat_orbitals, precision=HIGH).reshape(orbitals.shape)
    return (image, residual)


def solution(mesh):
    return jax.shard_map(
        on_device,
        mesh=mesh,
        in_specs=(
            P(None, "gz", "gy", "gx"),
            P("gz", "gy", "gx"),
            P("gz", "gy", "gx", None),
            P("gz", "gy", "gx", None, None),
            P("gz", "gy", "gx"),
            P("gz", "gy", "gx", None, None, None),
            P(),
        ),
        out_specs=(P(None, "gz", "gy", "gx"), P(None, "gz", "gy", "gx")),
        check_vma=False,
    )
```

profile of v0, /device:TPU:1, one launch (start us, length us, event | category | flops | bytes accessed | tf_op | source)
XLA Modules:
  0.0 696.8 jit_solution(14658654156391539896)
XLA Ops:
  7.2 0.0 copy-start
  7.2 0.0 copy-start.2
  7.2 0.0 all-reduce.2.cloned.1.call-start
  7.2 0.7 fusion.42
  7.9 1.5 copy.27
  9.4 0.0 copy-done.2
  10.1 5.5 gather_fusion
  15.5 0.0 copy-done
  15.5 1.8 fusion.1
  17.3 3.2 broadcast_in_dim.48
  20.5 2.1 scatter_fusion
  22.6 0.0 copy-start.1
  22.6 0.0 copy-start.5
  22.6 0.0 all-reduce.2.cloned.1.call-update
  22.7 0.8 copy-done.1
  23.5 0.1 constant_dynamic-update-slice_fusion.1
  23.5 0.1 fusion.46
  23.6 11.5 %collective-permute-start = (f32[4,4,8,4]{3,0,2,1:T(4,128)S(1)}, f32[4,4,8,4]{3,0,2,1:T(4,128)S(1)}, u32[]{:S(2)}, u32[]{:S(2)}) collective-permute-start(f32[4,4,8,4]{3,0,2,1:T(4,128)S(1)} %get-tuple-element.11), channel_id=1, source_target_pairs={{0,256},{256,512},{512,768},{768,0},{1,257},{257,513},{513,769},{7... | collective-permute-start | bytes 6152 | tf_op jit(solution)/shard_map/ppermute | solution.py:20
  35.1 9.1 %collective-permute-start.1 = (f32[4,4,8,4]{3,0,2,1:T(4,128)S(1)}, f32[4,4,8,4]{3,0,2,1:T(4,128)S(1)}, u32[]{:S(2)}, u32[]{:S(2)}) collective-permute-start(f32[4,4,8,4]{3,0,2,1:T(4,128)S(1)} %get-tuple-element.10), channel_id=1, source_target_pairs={{256,0},{512,256},{768,512},{0,768},{257,1},{513,257},{769,513},{1... | collective-permute-start | bytes 6152 | tf_op jit(solution)/shard_map/ppermute | solution.py:22
  44.3 0.0 copy-done.5
  44.3 0.0 copy-done.4
  44.4 0.0 collective-permute-done
  44.4 3.1 collective-permute-done.1
  47.5 0.2 pad_maximum_fusion.2
  47.7 7.4 %collective-permute-start.3 = (f32[4,4,4,136]{3,0,2,1:T(4,128)S(1)}, f32[4,4,4,136]{3,0,2,1:T(4,128)S(1)}, u32[]{:S(2)}, u32[]{:S(2)}) collective-permute-start(f32[4,4,4,136]{3,0,2,1:T(4,128)S(1)} %get-tuple-element.8), channel_id=1, source_target_pairs={{32,0},{64,32},{96,64},{128,96},{160,128},{192,160},{224,192},{0,2... | collective-permute-start | bytes 104456 | tf_op jit(solution)/shard_map/ppermute | solution.py:22
  55.1 2.5 collective-permute-start.2
  57.7 0.5 collective-permute-done.3
  58.2 0.7 collective-permute-done.2
  59.0 0.9 pad_maximum_fusion
  59.8 3.1 collective-permute-start.5
  63.0 6.2 collective-permute-start.4
  69.1 0.3 pad_maximum_fusion.1
  69.4 474.6 %all-reduce.2.cloned.1.call-done = f32[3072,8,4]{1,2,0:T(4,128)} async-done(((f32[3072,8,4]{1,2,0:T(4,128)}), f32[3072,8,4]{1,2,0:T(4,128)}) %all-reduce.2.cloned.1.call-update) | async-done | bytes 393232 | tf_op jit(solution)/shard_map/psum | solution.py:79
  544.0 3.4 gather_fusion.1
  547.4 0.3 fusion.31
  547.7 0.3 fusion
  548.0 1.3 copy.28
  549.3 12.3 %scatter_custom_fusion.1 = f32[4,4096]{0,1:T(8,128)S(1)} fusion(s32[2048]{0:T(1024)S(1)} %bitcast.61, f32[2048,4]{1,0:T(8,128)} %copy.28, f32[]{:T(128)} %constant.18.clone.1), kind=kCustom, calls=%fused_computation.10 | custom fusion | flops 8192 | bytes 66048 | tf_op jit(solution)/shard_map/scatter-add | solution.py:87
  561.7 0.6 copy.30
  562.3 0.0 collective-permute-done.5
  562.3 0.0 collective-permute-done.4
  562.3 0.0 copy-done.3
  562.3 2.1 add_add_fusion
  564.4 0.4 convolution_bitcast_fusion
  564.7 0.7 copy.32
  565.4 123.7 %psum.15 = f32[4,4]{0,1:T(4,128)S(1)} all-reduce(f32[4,4]{0,1:T(4,128)S(1)} %convolution_bitcast_fusion), channel_id=1, replica_groups=mesh['gx'=4,'gy'=8,'gz'=32] {'gx','gy','gz'}, use_global_device_ids=true, to_apply=%region_3.4 | all-reduce | flops 16 | bytes 128 | tf_op jit(solution)/shard_map/psum | solution.py:93
  689.1 0.3 convolution_subtract_fusion
  689.3 0.6 copy.33
  (10 shorter events, 0.1 us)
Async XLA Ops:
  7.2 8.4 %copy-start = (f32[1,1,1,16,8,128]{5,4,3,2,1,0:T(8,128)S(1)}, f32[1,1,1,16,8,128]{5,4,3,2,1,0:T(8,128)}, u32[]{:S(2)}) copy-start(f32[1,1,1,16,8,128]{5,4,3,2,1,0:T(8,128)} %param.12) | copy-start | bytes 196612
  7.2 2.2 copy-start.2
  7.2 536.8 %all-reduce.2.cloned.1.call-start = ((), (), s32[]{:S(2)}) async-start(), calls=%async_computation | async-start | bytes 12582912 | tf_op jit(solution)/shard_map/psum | solution.py:79
  22.6 0.8 copy-start.1
  22.6 21.6 %copy-start.5 = (s32[1,1,1,16]{3,2,1,0:T(1,128)S(1)}, s32[1,1,1,16]{3,2,1,0:T(1,128)}, u32[]{:S(2)}) copy-start(s32[1,1,1,16]{3,2,1,0:T(1,128)} %param.9) | copy-start | bytes 196
  22.6 21.7 %copy-start.4 = (f32[2,8,8]{2,1,0:T(8,128)S(1)}, f32[2,8,8]{2,1,0:T(8,128)}, u32[]{:S(2)}) copy-start(f32[2,8,8]{2,1,0:T(8,128)} %param.13) | copy-start | bytes 1540
  23.6 20.7 %collective-permute-start = (f32[4,4,8,4]{3,0,2,1:T(4,128)S(1)}, f32[4,4,8,4]{3,0,2,1:T(4,128)S(1)}, u32[]{:S(2)}, u32[]{:S(2)}) collective-permute-start(f32[4,4,8,4]{3,0,2,1:T(4,128)S(1)} %get-tuple-element.11), channel_id=1, source_target_pairs={{0,256},{256,512},{512,768},{768,0},{1,257},{257,513},{513,769},{7... | collective-permute-start | bytes 6152 | tf_op jit(solution)/shard_map/ppermute | solution.py:20
  35.1 12.4 %collective-permute-start.1 = (f32[4,4,8,4]{3,0,2,1:T(4,128)S(1)}, f32[4,4,8,4]{3,0,2,1:T(4,128)S(1)}, u32[]{:S(2)}, u32[]{:S(2)}) collective-permute-start(f32[4,4,8,4]{3,0,2,1:T(4,128)S(1)} %get-tuple-element.10), channel_id=1, source_target_pairs={{256,0},{512,256},{768,512},{0,768},{257,1},{513,257},{769,513},{1... | collective-permute-start | bytes 6152 | tf_op jit(solution)/shard_map/ppermute | solution.py:22
  47.7 10.5 %collective-permute-start.3 = (f32[4,4,4,136]{3,0,2,1:T(4,128)S(1)}, f32[4,4,4,136]{3,0,2,1:T(4,128)S(1)}, u32[]{:S(2)}, u32[]{:S(2)}) collective-permute-start(f32[4,4,4,136]{3,0,2,1:T(4,128)S(1)} %get-tuple-element.8), channel_id=1, source_target_pairs={{32,0},{64,32},{96,64},{128,96},{160,128},{192,160},{224,192},{0,2... | collective-permute-start | bytes 104456 | tf_op jit(solution)/shard_map/ppermute | solution.py:22
  55.1 3.8 collective-permute-start.2
  59.8 502.4 %collective-permute-start.5 = (f32[4,4,16,136]{3,0,2,1:T(4,128)}, f32[4,4,16,136]{3,0,2,1:T(4,128)S(1)}, u32[]{:S(2)}, u32[]{:S(2)}) collective-permute-start(f32[4,4,16,136]{3,0,2,1:T(4,128)} %pad_maximum_fusion), channel_id=1, source_target_pairs={{0,1},{1,2},{2,3},{3,4},{4,5},{5,6},{6,7},{7,8},{8,9},{9,10},{10,1... | collective-permute-start | bytes 417800 | tf_op jit(solution)/shard_map/ppermute | solution.py:20
  63.0 499.3 %collective-permute-start.4 = (f32[4,4,16,136]{3,0,2,1:T(4,128)}, f32[4,4,16,136]{3,0,2,1:T(4,128)}, u32[]{:S(2)}, u32[]{:S(2)}) collective-permute-start(f32[4,4,16,136]{3,0,2,1:T(4,128)} %pad_maximum_fusion), channel_id=1, source_target_pairs={{1,0},{2,1},{3,2},{4,3},{5,4},{6,5},{7,6},{8,7},{9,8},{10,9},{11,1... | collective-permute-start | bytes 417800 | tf_op jit(solution)/shard_map/ppermute | solution.py:22
  549.3 13.0 %copy-start.3 = (f32[4,8,128]{2,1,0:T(8,128)S(1)}, f32[4,8,128]{2,1,0:T(8,128)}, u32[]{:S(2)}) copy-start(f32[4,8,128]{2,1,0:T(8,128)} %param.8) | copy-start | bytes 49156
Sparse Core Ops, SparseCore 0:
  22.8 521.1 all-reduce.1
where the time goes:
time: 697 us
  waiting for transfers between devices  479 us (69%)
  blocking collectives  124 us (18%)
  starting transfers between devices  39.9 us (6%)
  other arithmetic  18.5 us (3%)
  local copies, waits for them, and re-layouts  17.8 us (3%)
  between operations  14.9 us (2%)
    psum x1, waiting for transfers between devices, on_device(): totals = lax.psum(dense_sums, ('gx', 'gy', 'gz'))  475 us
    psum x1, blocking collectives, on_device(): lax.psum(jnp.dot(flat_orbitals, flat_image.T, precision=HIGH), ('gx', 'gy...  124 us
    ppermute x3, starting transfers between devices, padded_2(): lax.ppermute(head, axis, [((i + 1) % count, i) for i in range(count)])  22.7 us
    ppermute x3, starting transfers between devices, padded_2(): lax.ppermute(tail, axis, [(i, (i + 1) % count) for i in range(count)])  17.1 us
  transfers between devices with their start and end apart: 7, of which 4 were waited for; matrix products, arithmetic and copies ran while one was open for 3% of the time, Pallas kernels for 0%

commit v1 on v0

v1 whole, which is shorter than its diff:
```python
import jax
import jax.numpy as jnp
from jax import lax
from jax.experimental import pallas as pl
from jax.experimental.pallas import tpu as pltpu
from jax.sharding import PartitionSpec as P

MESH = pl.DeviceIdType.MESH
HIGH = lax.Precision.HIGHEST
SIZES = (4, 8, 32)
GRID_TOTAL = 4194304
STENCIL = (-205.0 / 72.0, 8.0 / 5.0, -1.0 / 5.0, 8.0 / 315.0, -1.0 / 560.0)
KIN = tuple(-0.5 * c for c in STENCIL)
DIRS = [(d % 3 - 1, d // 3 % 3 - 1, d // 9 - 1) for d in range(27)]
OTHERS = [d for d in range(27) if d != 13]
PAIRS = [(i, j) for j in range(4) for i in range(j + 1)]
HALOS = [(0, 0, 1), (0, 0, -1), (0, 1, 0), (0, -1, 0), (1, 0, 0), (-1, 0, 0)]


def here():
    return lax.axis_index("gx"), lax.axis_index("gy"), lax.axis_index("gz")


def at_offset(delta):
    return tuple(
        v if d % n == 0 else (v + (d % n)) & (n - 1) for v, d, n in zip(here(), delta, SIZES)
    )


PLANE = [(0, 0, d) for d in range(1, 32)]
COLUMN = [(dx, dy, 0) for dx in range(4) for dy in range(8) if (dx, dy) != (0, 0)]


def all_partners():
    wanted = [DIRS[d] for d in OTHERS] + PLANE + COLUMN
    seen = []
    for delta in wanted:
        key = tuple(d % n for d, n in zip(delta, SIZES))
        if key not in seen:
            seen.append(key)
    return seen


def lanes(shape):
    return lax.broadcasted_iota(jnp.int32, shape, len(shape) - 1)


def sublanes(shape):
    return lax.broadcasted_iota(jnp.int32, shape, len(shape) - 2)


def row_sum(v):
    total = v[0:8]
    for k in range(8, v.shape[0], 8):
        total = total + v[k : k + 8]
    for shift in (4, 2, 1):
        total = total + pltpu.roll(total, shift, 0)
    return total


def main_kernel(
    orb_hbm, pot_hbm, atom_hbm, points_hbm, count_hbm, beta_hbm, coup_hbm,
    image_ref, gram_ref,
    psi, pot, pts, beta, coup, atom, count,
    zb, hy, pk, xb, msg, r1, a2, arow, sa, ba, sb, bb, rows16, onehot, spread,
    lsem, hsend, hrecv, csend, crecv,
):
    orb, ptsb = orb_hbm, points_hbm.at[0, 0, 0]
    loads = [
        pltpu.make_async_copy(orb, psi, lsem.at[0]),
        pltpu.make_async_copy(ptsb, pts, lsem.at[1]),
        pltpu.make_async_copy(beta_hbm.at[0, 0, 0], beta, lsem.at[2]),
        pltpu.make_async_copy(atom_hbm, atom, lsem.at[3]),
        pltpu.make_async_copy(count_hbm, count, lsem.at[4]),
        pltpu.make_async_copy(coup_hbm, coup, lsem.at[5]),
        pltpu.make_async_copy(pot_hbm, pot, lsem.at[6]),
    ]
    for load in loads:
        load.start()
    barrier = pltpu.get_barrier_semaphore()
    partners = all_partners()
    for delta in partners:
        pl.semaphore_signal(barrier, inc=1, device_id=at_offset(delta), device_id_type=MESH)

    def remote(src, dst, send, recv, delta):
        return pltpu.make_async_remote_copy(
            src_ref=src, dst_ref=dst, send_sem=send, recv_sem=recv,
            device_id=at_offset(delta), device_id_type=MESH,
        )

    def wait_bytes(ref, sem):
        pltpu.make_async_copy(ref, ref, sem).wait()

    lane8, sub8 = lanes((8, 128)), sublanes((8, 128))
    loads[0].wait()
    loads[1].wait()

    packed = jnp.zeros((8, 128), jnp.float32)
    for n in range(4):
        for z in range(4):
            g = n * 4 + z
            moved = pltpu.roll(psi[n, z], (4 + 8 * g) % 128, 1)
            packed = jnp.where(lane8 // 8 == g, moved, packed)
    pk[...] = packed

    lo = [pts[8 * h : 8 * h + 8] & 127 for h in range(2)]
    hi = [pts[8 * h : 8 * h + 8] >> 7 for h in range(2)]
    gathered = [[jnp.zeros((8, 128), jnp.float32) for _ in range(2)] for _ in range(4)]
    for row in range(32):
        pick = [hi[h] == row for h in range(2)]
        for n in range(4):
            line = jnp.broadcast_to(psi[n, row // 8, row % 8 : row % 8 + 1], (8, 128))
            for h in range(2):
                got = jnp.take_along_axis(line, lo[h], axis=1)
                gathered[n][h] = jnp.where(pick[h], got, gathered[n][h])

    for load in loads[2:]:
        load.wait()
    x, y, z = here()
    slots = count[0, 0, 0]
    dir_of, kind_of = [], []
    for b in range(16):
        a = atom[0, 0, 0, b]
        owner = a // 3
        dx = ((owner & 3) - x + 1) & 3
        dy = (((owner >> 2) & 7) - y + 1) & 7
        dz = ((owner >> 5) - z + 1) & 31
        where = jnp.minimum(jnp.maximum(dz * 9 + dy * 3 + dx, 0), 26)
        dir_of.append(where)
        kind_of.append(a - owner * 3)
    dir_lane = jnp.full((32, 128), 31, jnp.int32)
    for b in range(16):
        used = jnp.where(b < slots, dir_of[b], 31)
        dir_lane = jnp.where(lanes((32, 128)) // 8 == b, used, dir_lane)
    select = (sublanes((32, 128)) == dir_lane).astype(jnp.float32)

    lane_n, lane_k, lane_p = lane8 // 32, (lane8 // 8) & 3, lane8 & 7
    blocks = []
    for b in range(16):
        block = jnp.zeros((8, 128), jnp.float32)
        for n in range(4):
            line = jnp.broadcast_to(gathered[n][b // 8][b % 8 : b % 8 + 1], (8, 128))
            part = jnp.sum(beta[b] * line, axis=1, keepdims=True)
            block = jnp.where(lane_n == n, part, block)
        keep = (lane_p == sub8) & (lane_k == kind_of[b])
        blocks.append(jnp.where(keep, block, 0.0))
    msg[...] = jnp.dot(
        select, jnp.concatenate(blocks, axis=0), precision=HIGH, preferred_element_type=jnp.float32
    )

    pl.semaphore_wait(barrier, len(partners))
    for d in OTHERS:
        remote(msg.at[pl.ds(d, 1)], r1.at[pl.ds(d, 1)], csend.at[0], crecv.at[0], DIRS[d]).start()
    halo_copies = [
        (psi, zb.at[0]),
        (psi, zb.at[1]),
        (psi.at[:, :, pl.ds(4, 4)], hy.at[:, :, pl.ds(4, 4)]),
        (psi.at[:, :, pl.ds(0, 4)], hy.at[:, :, pl.ds(0, 4)]),
        (pk, xb.at[0]),
        (pk, xb.at[1]),
    ]
    halos = [
        remote(src, dst, hsend.at[k], hrecv.at[k], HALOS[k])
        for k, (src, dst) in reversed(list(enumerate(halo_copies)))
    ]
    for halo in halos:
        halo.start()
    r1[pl.ds(13, 1)] = msg[pl.ds(13, 1)]
    r1[pl.ds(27, 5)] = jnp.zeros((5, 128), jnp.float32)

    tiles = []
    for c in range(2):
        tile = jnp.concatenate([coup[c], jnp.zeros((8, 120), jnp.float32)], axis=1)
        for shift in (8, 16, 32, 64):
            tile = tile + pltpu.roll(tile, shift, 1)
        tiles.append(tile)
    couple = jnp.concatenate(
        [jnp.where(lane8 // 8 == r, tiles[0 if r % 4 == 0 else 1], 0.0) for r in range(16)], axis=0
    )
    li, si = lanes((128, 128)), sublanes((128, 128))
    away = (li - si) & 127
    away = jnp.minimum(away, 128 - away)
    along_x = jnp.where(away == 0, 3.0 * KIN[0], 0.0)
    for o in range(1, 5):
        along_x = jnp.where(away == o, KIN[o], along_x)
    sj, lj = si & 7, li & 7
    edge = jnp.zeros((128, 128), jnp.float32)
    for o in range(1, 5):
        left = (sj < 4) & (lj >= 4) & (lj - sj == o)
        right = (sj >= 4) & (lj < 4) & (sj - lj == o)
        edge = jnp.where((si // 8 == li // 8) & (left | right), KIN[o], edge)

    flat = psi[...].reshape(128, 128)
    base = jnp.dot(flat, along_x, precision=HIGH, preferred_element_type=jnp.float32)

    for b in range(16):
        line = jnp.broadcast_to(lo[b // 8][b % 8 : b % 8 + 1], (128, 128))
        onehot[:, pl.ds(b * 128, 128)] = (si == line).astype(jnp.bfloat16)

    for halo in halos:
        halo.wait_recv()
    change = jnp.where(lane8 & 7 < 4, xb[0], xb[1]) - pk[...]
    change = jnp.dot(change, edge, precision=HIGH, preferred_element_type=jnp.float32)
    at_edge = (lane8 < 4) | (lane8 >= 124)
    sums = [None] * len(PAIRS)
    for zz in range(4):
        image = []
        for n in range(4):
            own, other = psi[n, zz], hy[n, zz]
            total = base[(n * 4 + zz) * 8 : (n * 4 + zz) * 8 + 8]
            moved = pltpu.roll(change, (124 - 8 * (n * 4 + zz)) % 128, 1)
            total = total + jnp.where(at_edge, moved, 0.0)
            for o in range(1, 5):
                up = psi[n, zz + o] if zz + o < 4 else zb[1, n, zz + o - 4]
                down = psi[n, zz - o] if zz - o >= 0 else zb[0, n, zz - o + 4]
                before = pltpu.roll(jnp.where(sub8 < 8 - o, own, other), o, 0)
                after = pltpu.roll(jnp.where(sub8 >= o, own, other), 8 - o, 0)
                total = total + KIN[o] * ((up + down) + (before + after))
            total = total + pot[zz] * own
            image.append(total)
            image_ref[n, zz] = total
        for k, (i, j) in enumerate(PAIRS):
            term = psi[i, zz] * image[j]
            sums[k] = term if sums[k] is None else sums[k] + term
    local = jnp.zeros((8, 128), jnp.float32)
    for k, (i, j) in enumerate(PAIRS):
        total = jnp.sum(sums[k], axis=1, keepdims=True)
        local = jnp.where(lane8 == j * 32 + (j - i) * 8, total, local)

    wait_bytes(r1.at[pl.ds(0, 26)], crecv.at[0])
    coef = row_sum(r1[...])
    applied = jnp.dot(coef, couple, precision=HIGH, preferred_element_type=jnp.float32)
    arow[...] = applied
    turned = coef
    for s in range(1, 4):
        turned = jnp.where(sub8 == s, pltpu.roll(coef, 32 * s, 1), turned)
    outer = turned * applied
    outer = outer + (pltpu.roll(outer, 120, 1) + pltpu.roll(outer, 112, 1))
    outer = jnp.where((sub8 < 4) & (lane8 & 31 < 8), outer, 0.0)
    placed = local
    for s in range(4):
        placed = placed + jnp.where(sub8 == s, pltpu.roll(outer, 8 * s, 1) if s else outer, 0.0)
    placed = row_sum(placed)
    sa[...] = placed

    for k, delta in enumerate(PLANE):
        remote(sa.at[pl.ds(0, 1)], ba.at[pl.ds(k, 1)], csend.at[2], crecv.at[2], delta).start()
    for d in OTHERS:
        remote(arow.at[pl.ds(0, 1)], a2.at[pl.ds(26 - d, 1)], csend.at[1], crecv.at[1], DIRS[d]).start()
    a2[pl.ds(13, 1)] = arow[pl.ds(0, 1)]
    ba[pl.ds(31, 1)] = sa[pl.ds(0, 1)]
    wait_bytes(ba.at[pl.ds(0, 31)], crecv.at[2])
    sb[...] = row_sum(ba[...])
    for k, delta in enumerate(COLUMN):
        remote(sb.at[pl.ds(0, 1)], bb.at[pl.ds(k, 1)], csend.at[3], crecv.at[3], delta).start()
    bb[pl.ds(31, 1)] = sb[pl.ds(0, 1)]

    wait_bytes(a2.at[pl.ds(0, 26)], crecv.at[1])
    for b in range(16):
        rows16[pl.ds(b, 1)] = a2[pl.ds(dir_of[b], 1)]
    spots = []
    for h in range(2):
        kind = jnp.zeros((8, 128), jnp.int32)
        for b in range(8):
            kind = jnp.where(sub8 == b, kind_of[h * 8 + b], kind)
        spots.append(kind * 8 + lane_p)
    left = []
    for n in range(4):
        for h in range(2):
            got = jnp.take_along_axis(rows16[pl.ds(h * 8, 8)], spots[h] + 32 * n, axis=1)
            slot = sub8 + 8 * h
            left.append(jnp.where((lane8 // 8 == slot) & (slot < slots), got, 0.0))
    values = jnp.dot(
        jnp.concatenate(left, axis=0), beta[...].reshape(128, 128), precision=HIGH,
        preferred_element_type=jnp.float32,
    )
    high = values.astype(jnp.bfloat16).astype(jnp.float32)
    low = values - high
    for b in range(16):
        line = jnp.broadcast_to(hi[b // 8][b % 8 : b % 8 + 1], (32, 128))
        pick = sublanes((32, 128)) == line
        for part, source in enumerate((high, low)):
            for n in range(4):
                r = n * 16 + b
                piece = jnp.where(pick, jnp.broadcast_to(source[r : r + 1], (32, 128)), 0.0)
                spread[pl.ds(part * 128 + n * 32, 32), pl.ds(b * 128, 128)] = piece.astype(jnp.bfloat16)
    grid = lax.dot_general(
        spread[...], onehot[...], (((1,), (1,)), ((), ())), preferred_element_type=jnp.float32
    )
    projected = grid[0:128] + grid[128:256]
    image_ref[...] = image_ref[...] + projected.reshape(4, 4, 8, 128)

    wait_bytes(bb.at[pl.ds(0, 31)], crecv.at[3])
    gram_ref[...] = row_sum(bb[...])
    for halo in halos:
        halo.wait_send()
    wait_bytes(r1.at[pl.ds(0, 26)], csend.at[0])
    wait_bytes(a2.at[pl.ds(0, 26)], csend.at[1])
    wait_bytes(ba.at[pl.ds(0, 31)], csend.at[2])
    wait_bytes(bb.at[pl.ds(0, 31)], csend.at[3])


def residual_kernel(psi, image, gram, image_out, residual_out):
    lane8 = lanes((8, 128))
    row = gram[...]
    weight = {}
    for i, j in PAIRS:
        group = j * 4 + (j - i)
        total = jnp.sum(jnp.where(lane8 // 8 == group, row, 0.0), axis=1, keepdims=True)
        total = jnp.broadcast_to(total, (8, 128)) * (1.0 / GRID_TOTAL)
        weight[i, j] = weight[j, i] = total
    for z in range(4):
        for j in range(4):
            total = image[j, z]
            image_out[j, z] = total
            for i in range(4):
                total = total - weight[i, j] * psi[i, z]
            residual_out[j, z] = total


def on_device(orbitals, potential, block_atom, block_points, block_count, projector_values, coupling):
    f32, i32 = jnp.float32, jnp.int32
    anywhere = pl.BlockSpec(memory_space=pl.ANY)
    vmem = pl.BlockSpec(memory_space=pltpu.VMEM)
    field = jax.ShapeDtypeStruct((4, 4, 8, 128), f32)
    image, gram = pl.pallas_call(
        main_kernel,
        out_shape=(field, jax.ShapeDtypeStruct((8, 128), f32)),
        in_specs=[anywhere] * 7,
        out_specs=(vmem, vmem),
        scratch_shapes=[
            pltpu.VMEM((4, 4, 8, 128), f32),
            pltpu.VMEM((4, 8, 128), f32),
            pltpu.VMEM((16, 128), i32),
            pltpu.VMEM((16, 8, 128), f32),
            pltpu.VMEM((2, 8, 8), f32),
            pltpu.SMEM((1, 1, 1, 16), i32),
            pltpu.SMEM((1, 1, 1), i32),
            pltpu.VMEM((2, 4, 4, 8, 128), f32),
            pltpu.VMEM((4, 4, 8, 128), f32),
            pltpu.VMEM((8, 128), f32),
            pltpu.VMEM((2, 8, 128), f32),
            pltpu.VMEM((32, 128), f32),
            pltpu.VMEM((32, 128), f32),
            pltpu.VMEM((32, 128), f32),
            pltpu.VMEM((8, 128), f32),
            pltpu.VMEM((8, 128), f32),
            pltpu.VMEM((32, 128), f32),
            pltpu.VMEM((8, 128), f32),
            pltpu.VMEM((32, 128), f32),
            pltpu.VMEM((16, 128), f32),
            pltpu.VMEM((128, 2048), jnp.bfloat16),
            pltpu.VMEM((256, 2048), jnp.bfloat16),
            pltpu.SemaphoreType.DMA((7,)),
            pltpu.SemaphoreType.DMA((6,)),
            pltpu.SemaphoreType.DMA((6,)),
            pltpu.SemaphoreType.DMA((4,)),
            pltpu.SemaphoreType.DMA((4,)),
        ],
        compiler_params=pltpu.CompilerParams(
            collective_id=0, has_side_effects=True, vmem_limit_bytes=24 * 1024 * 1024
        ),
    )(orbitals, potential, block_atom, block_points, block_count, projector_values, coupling)
    return pl.pallas_call(
        residual_kernel,
        out_shape=(field, field),
        in_specs=[vmem] * 3,
        out_specs=(vmem, vmem),
    )(orbitals, image, gram)


def solution(mesh):
    return jax.shard_map(
        on_device,
        mesh=mesh,
        in_specs=(
            P(None, "gz", "gy", "gx"),
            P("gz", "gy", "gx"),
            P("gz", "gy", "gx", None),
            P("gz", "gy", "gx", None, None),
            P("gz", "gy", "gx"),
            P("gz", "gy", "gx", None, None, None),
            P(),
        ),
        out_specs=(P(None, "gz", "gy", "gx"), P(None, "gz", "gy", "gx")),
        check_vma=False,
    )
```

time: 697 us -> 52.6 us (0.08)
  waiting for transfers between devices: 479 us -> 0 us
  blocking collectives: 124 us -> 0 us
  Pallas kernels: 0 us -> 45.9 us
  starting transfers between devices: 39.9 us -> 0 us
  other arithmetic: 18.5 us -> 0 us
  between operations: 14.9 us -> 1.34 us
  local copies, waits for them, and re-layouts: 17.8 us -> 5 us
    psum x1 -> x0, waiting for transfers between devices: 475 us -> none  [on_device(): totals = lax.psum(dense_sums, ('gx', 'gy', 'gz'))]
    psum x1 -> x0, blocking collectives: 124 us -> none  [on_device(): lax.psum(jnp.dot(flat_orbitals, flat_image.T, precision=HIGH), ('gx', 'gy...]
    pallas_call x0 -> x2, Pallas kernels: none -> 45.9 us  [the longest x1 44.3 us: on_device(): pl.pallas_call(main_kernel, out_shape=(field, jax.ShapeDtypeStruct((8, 12...]
    ppermute x6 -> x0, starting transfers between devices: 39.9 us -> none  [the longest x3 22.7 us: padded_2(): lax.ppermute(head, axis, [((i + 1) % count, i) for i in range(count)])]
    scatter-add x2 -> x0, other arithmetic: 14.4 us -> none  [the longest x1 12.3 us: on_device(): projected = jnp.zeros((orbital_count, points_total), jnp.float32).at[:, p...]
    gather x2 -> x0, local copies, waits for them, and re-layouts: 8.84 us -> none  [the longest x1 5.47 us: on_device(): gathered = flat_orbitals[:, points]]
  transfers between devices with their start and end apart: 7 -> 0, of which waited for: 4 -> 0; matrix products, arithmetic and copies ran while one was open for 3% -> 0% of each run, Pallas kernels for 0% -> 0%
where the time goes in v1:
time: 52.6 us; the launch traced here: 52.2 us
  Pallas kernels  45.9 us (87%)
  local copies, waits for them, and re-layouts  5 us (10%)
  between operations  1.34 us (3%)
    pallas_call x1, Pallas kernels, on_device(): pl.pallas_call(main_kernel, out_shape=(field, jax.ShapeDtypeStruct((8, 12...  44.3 us
    unnamed x16, local copies, waits for them, and re-layouts  5 us
    pallas_call x1, Pallas kernels, on_device(): pl.pallas_call(residual_kernel, out_shape=(field, field), in_specs=[vmem]...  1.61 us

profile of v1, /device:TPU:1, one launch (start us, length us, event | category | flops | bytes accessed | tf_op | source)
XLA Modules:
  0.0 52.2 jit_solution(5828083823712542057)
XLA Ops:
  0.6 0.0 copy-start.7
  1.3 0.0 copy-done.7
  1.3 0.0 copy-start
  1.3 0.8 %copy-done = f32[4,4,8,128]{3,2,1,0:T(8,128)S(1)} copy-done((f32[4,4,8,128]{3,2,1,0:T(8,128)S(1)}, f32[4,4,8,128]{3,2,1,0:T(8,128)}, u32[]{:S(2)}) %copy-start) | copy-done | bytes 65560
  2.2 0.0 copy-start.1
  2.2 0.8 %copy-done.1 = f32[1,1,1,16,8,128]{5,4,3,2,1,0:T(8,128)S(1)} copy-done((f32[1,1,1,16,8,128]{5,4,3,2,1,0:T(8,128)S(1)}, f32[1,1,1,16,8,128]{5,4,3,2,1,0:T(8,128)}, u32[]{:S(2)}) %copy-start.1) | copy-done | bytes 65560
  3.0 0.0 copy-start.3
  3.0 0.7 %copy-done.3 = f32[4,8,128]{2,1,0:T(8,128)S(1)} copy-done((f32[4,8,128]{2,1,0:T(8,128)S(1)}, f32[4,8,128]{2,1,0:T(8,128)}, u32[]{:S(2)}) %copy-start.3) | copy-done | bytes 16408
  3.7 0.0 copy-start.4
  3.7 0.7 %copy-done.4 = s32[1,1,1,16,128]{4,3,2,1,0:T(8,128)S(1)} copy-done((s32[1,1,1,16,128]{4,3,2,1,0:T(8,128)S(1)}, s32[1,1,1,16,128]{4,3,2,1,0:T(8,128)}, u32[]{:S(2)}) %copy-start.4) | copy-done | bytes 8216
  4.4 0.0 copy-start.5
  4.4 0.7 %copy-done.5 = f32[2,8,8]{2,1,0:T(8,128)S(1)} copy-done((f32[2,8,8]{2,1,0:T(8,128)S(1)}, f32[2,8,8]{2,1,0:T(8,128)}, u32[]{:S(2)}) %copy-start.5) | copy-done | bytes 536
  5.1 44.3 %shard_map.86 = (f32[4,4,8,128]{3,2,1,0:T(8,128)S(1)}, f32[8,128]{1,0:T(8,128)S(1)}) custom-call(f32[4,4,8,128]{3,2,1,0:T(8,128)S(1)} %copy-done, f32[4,8,128]{2,1,0:T(8,128)S(1)} %copy-done.3, s32[1,1,1,16]{3,2,1,0:T(1,128)S(1)} %copy-done.7, s32[1,1,1,16,128]{4,3,2,1,0:T(8,128)S(1)} %copy-done.4, s32[1,1,1]{2,1,0:T(1,128)S(6)} %copy.9.count_hbm, ...), custom_call_target="tpu_custom_call" | custom-call | tf_op jit(solution)/shard_map/pallas_call | solution.py:326
  49.4 0.0 copy-start.2
  49.4 0.6 %copy-done.2 = f32[4,4,8,128]{3,2,1,0:T(8,128)} copy-done((f32[4,4,8,128]{3,2,1,0:T(8,128)}, f32[4,4,8,128]{3,2,1,0:T(8,128)S(1)}, u32[]{:S(2)}) %copy-start.2) | copy-done | bytes 65560
  50.0 0.0 copy-start.6
  50.0 0.6 %copy-done.6 = f32[8,128]{1,0:T(8,128)} copy-done((f32[8,128]{1,0:T(8,128)}, f32[8,128]{1,0:T(8,128)S(1)}, u32[]{:S(2)}) %copy-start.6) | copy-done | bytes 4120
  50.6 1.6 %shard_map.87 = (f32[4,4,8,128]{3,2,1,0:T(8,128)}, f32[4,4,8,128]{3,2,1,0:T(8,128)}) custom-call(f32[4,4,8,128]{3,2,1,0:T(8,128)} %psi.1, f32[4,4,8,128]{3,2,1,0:T(8,128)} %copy-done.2, f32[8,128]{1,0:T(8,128)} %copy-done.6), custom_call_target="tpu_custom_call" | custom-call | tf_op jit(solution)/shard_map/pallas_call | solution.py:364
Async XLA Ops:
  0.6 0.7 %copy-start.7 = (s32[1,1,1,16]{3,2,1,0:T(1,128)S(1)}, s32[1,1,1,16]{3,2,1,0:T(1,128)}, u32[]{:S(2)}) copy-start(s32[1,1,1,16]{3,2,1,0:T(1,128)} %atom_hbm.1) | copy-start | bytes 196
  1.3 0.8 %copy-start = (f32[4,4,8,128]{3,2,1,0:T(8,128)S(1)}, f32[4,4,8,128]{3,2,1,0:T(8,128)}, u32[]{:S(2)}) copy-start(f32[4,4,8,128]{3,2,1,0:T(8,128)} %psi.1) | copy-start | bytes 196612
  2.2 0.8 %copy-start.1 = (f32[1,1,1,16,8,128]{5,4,3,2,1,0:T(8,128)S(1)}, f32[1,1,1,16,8,128]{5,4,3,2,1,0:T(8,128)}, u32[]{:S(2)}) copy-start(f32[1,1,1,16,8,128]{5,4,3,2,1,0:T(8,128)} %beta_hbm.1) | copy-start | bytes 196612
  3.0 0.7 %copy-start.3 = (f32[4,8,128]{2,1,0:T(8,128)S(1)}, f32[4,8,128]{2,1,0:T(8,128)}, u32[]{:S(2)}) copy-start(f32[4,8,128]{2,1,0:T(8,128)} %pot_hbm.1) | copy-start | bytes 49156
  3.7 0.7 %copy-start.4 = (s32[1,1,1,16,128]{4,3,2,1,0:T(8,128)S(1)}, s32[1,1,1,16,128]{4,3,2,1,0:T(8,128)}, u32[]{:S(2)}) copy-start(s32[1,1,1,16,128]{4,3,2,1,0:T(8,128)} %points_hbm.1) | copy-start | bytes 24580
  4.4 0.7 %copy-start.5 = (f32[2,8,8]{2,1,0:T(8,128)S(1)}, f32[2,8,8]{2,1,0:T(8,128)}, u32[]{:S(2)}) copy-start(f32[2,8,8]{2,1,0:T(8,128)} %coup_hbm.1) | copy-start | bytes 1540
  49.4 0.6 %copy-start.2 = (f32[4,4,8,128]{3,2,1,0:T(8,128)}, f32[4,4,8,128]{3,2,1,0:T(8,128)S(1)}, u32[]{:S(2)}) copy-start(f32[4,4,8,128]{3,2,1,0:T(8,128)S(1)} %get-tuple-element.4.image) | copy-start | bytes 196612
  50.0 0.6 %copy-start.6 = (f32[8,128]{1,0:T(8,128)}, f32[8,128]{1,0:T(8,128)S(1)}, u32[]{:S(2)}) copy-start(f32[8,128]{1,0:T(8,128)S(1)} %get-tuple-element.5.gram) | copy-start | bytes 12292

commit v2 on v1

--- a/solution.py
+++ b/solution.py
@@ -61,7 +61,7 @@
 def main_kernel(
     orb_hbm, pot_hbm, atom_hbm, points_hbm, count_hbm, beta_hbm, coup_hbm,
     image_ref, gram_ref,
-    psi, pot, pts, beta, coup, atom, count,
+    psi, pot, pts, beta, coup, atom,
     zb, hy, pk, xb, msg, r1, a2, arow, sa, ba, sb, bb, rows16, onehot, spread,
     lsem, hsend, hrecv, csend, crecv,
 ):
@@ -71,7 +71,6 @@
         pltpu.make_async_copy(ptsb, pts, lsem.at[1]),
         pltpu.make_async_copy(beta_hbm.at[0, 0, 0], beta, lsem.at[2]),
         pltpu.make_async_copy(atom_hbm, atom, lsem.at[3]),
-        pltpu.make_async_copy(count_hbm, count, lsem.at[4]),
         pltpu.make_async_copy(coup_hbm, coup, lsem.at[5]),
         pltpu.make_async_copy(pot_hbm, pot, lsem.at[6]),
     ]
@@ -117,7 +116,7 @@
     for load in loads[2:]:
         load.wait()
     x, y, z = here()
-    slots = count[0, 0, 0]
+    slots = count_hbm[0, 0, 0]
     dir_of, kind_of = [], []
     for b in range(16):
         a = atom[0, 0, 0, b]
@@ -300,7 +299,9 @@
     wait_bytes(bb.at[pl.ds(0, 31)], csend.at[3])
 
 
-def residual_kernel(psi, image, gram, image_out, residual_out):
+def residual_kernel(psi, image, gram, image_out, residual_out, residual, sem):
+    copies = [pltpu.make_async_copy(image, image_out, sem.at[4])]
+    copies[0].start()
     lane8 = lanes((8, 128))
     row = gram[...]
     weight = {}
@@ -309,24 +310,32 @@
         total = jnp.sum(jnp.where(lane8 // 8 == group, row, 0.0), axis=1, keepdims=True)
         total = jnp.broadcast_to(total, (8, 128)) * (1.0 / GRID_TOTAL)
         weight[i, j] = weight[j, i] = total
-    for z in range(4):
-        for j in range(4):
+    for j in range(4):
+        for z in range(4):
             total = image[j, z]
-            image_out[j, z] = total
             for i in range(4):
                 total = total - weight[i, j] * psi[i, z]
-            residual_out[j, z] = total
+            residual[j, z] = total
+        copies.append(pltpu.make_async_copy(residual.at[j], residual_out.at[j], sem.at[j]))
+        copies[-1].start()
+    for copy in copies:
+        copy.wait()
 
 
 def on_device(orbitals, potential, block_atom, block_points, block_count, projector_values, coupling):
     f32, i32 = jnp.float32, jnp.int32
-    anywhere = pl.BlockSpec(memory_space=pl.ANY)
+    hbm = pl.BlockSpec(memory_space=pl.ANY)
     vmem = pl.BlockSpec(memory_space=pltpu.VMEM)
     field = jax.ShapeDtypeStruct((4, 4, 8, 128), f32)
+    held = [
+        pltpu.with_memory_space_constraint(v, pltpu.HBM)
+        for v in (orbitals, potential, block_atom, block_points, projector_values, coupling)
+    ]
+    held.insert(4, block_count)
     image, gram = pl.pallas_call(
         main_kernel,
-        out_shape=(field, jax.ShapeDtypeStruct((8, 128), f32)),
-        in_specs=[anywhere] * 7,
+        out_shape=(pltpu.VMEM((4, 4, 8, 128), f32), pltpu.VMEM((8, 128), f32)),
+        in_specs=[hbm] * 4 + [pl.BlockSpec(memory_space=pltpu.SMEM)] + [hbm] * 2,
         out_specs=(vmem, vmem),
         scratch_shapes=[
             pltpu.VMEM((4, 4, 8, 128), f32),
@@ -335,7 +344,6 @@
             pltpu.VMEM((16, 8, 128), f32),
             pltpu.VMEM((2, 8, 8), f32),
             pltpu.SMEM((1, 1, 1, 16), i32),
-            pltpu.SMEM((1, 1, 1), i32),
             pltpu.VMEM((2, 4, 4, 8, 128), f32),
             pltpu.VMEM((4, 4, 8, 128), f32),
             pltpu.VMEM((8, 128), f32),
@@ -360,12 +368,14 @@
         compiler_params=pltpu.CompilerParams(
             collective_id=0, has_side_effects=True, vmem_limit_bytes=24 * 1024 * 1024
         ),
-    )(orbitals, potential, block_atom, block_points, block_count, projector_values, coupling)
+    )(*held)
     return pl.pallas_call(
         residual_kernel,
         out_shape=(field, field),
         in_specs=[vmem] * 3,
-        out_specs=(vmem, vmem),
+        out_specs=(hbm, hbm),
+        scratch_shapes=[pltpu.VMEM((4, 4, 8, 128), f32), pltpu.SemaphoreType.DMA((5,))],
+        compiler_params=pltpu.CompilerParams(vmem_limit_bytes=16 * 1024 * 1024),
     )(orbitals, image, gram)
 
 

time: 52.6 us -> 46.5 us (0.88)
  local copies, waits for them, and re-layouts: 5 us -> 0.01 us
  Pallas kernels: 45.9 us -> 45 us
    unnamed x16 -> x2, local copies, waits for them, and re-layouts: 5 us -> 0.01 us
    pallas_call x1, Pallas kernels: 1.61 us -> 0.77 us  [on_device(): pl.pallas_call(residual_kernel, out_shape=(field, field), in_specs=[vmem]...]
where the time goes in v2:
time: 46.5 us; the launch traced here: 46.3 us
  Pallas kernels  45 us (97%)
  between operations  1.3 us (3%)
    pallas_call x1, Pallas kernels, on_device(): pl.pallas_call(main_kernel, out_shape=(pltpu.VMEM((4, 4, 8, 128), f32), p...  44.2 us

profile of v2, /device:TPU:1, one launch (start us, length us, event | category | flops | bytes accessed | tf_op | source)
XLA Modules:
  0.0 46.3 jit_solution(3225398107896045154)
XLA Ops:
  1.3 0.0 copy-start
  1.3 44.2 %shard_map.86 = (f32[4,4,8,128]{3,2,1,0:T(8,128)S(1)}, f32[8,128]{1,0:T(8,128)S(1)}) custom-call(f32[4,4,8,128]{3,2,1,0:T(8,128)} %psi.1, f32[4,8,128]{2,1,0:T(8,128)} %pot_hbm.1, s32[1,1,1,16]{3,2,1,0:T(1,128)} %atom_hbm.1, s32[1,1,1,16,128]{4,3,2,1,0:T(8,128)} %points_hbm.1, s32[1,1,1]{2,1,0:T(1,128)S(6)} %copy.9.count_hbm, ...), custom_call_target="tpu_custom_call" | custom-call | tf_op jit(solution)/shard_map/pallas_call | solution.py:335
  45.5 0.0 copy-done
  45.5 0.8 %shard_map.87 = (f32[4,4,8,128]{3,2,1,0:T(8,128)}, f32[4,4,8,128]{3,2,1,0:T(8,128)}) custom-call(f32[4,4,8,128]{3,2,1,0:T(8,128)S(1)} %copy-done, f32[4,4,8,128]{3,2,1,0:T(8,128)S(1)} %get-tuple-element.4.image, f32[8,128]{1,0:T(8,128)S(1)} %get-tuple-element.5.gram), custom_call_target="tpu_custom_call" | custom-call | tf_op jit(solution)/shard_map/pallas_call | solution.py:372
Async XLA Ops:
  1.3 44.2 %copy-start = (f32[4,4,8,128]{3,2,1,0:T(8,128)S(1)}, f32[4,4,8,128]{3,2,1,0:T(8,128)}, u32[]{:S(2)}) copy-start(f32[4,4,8,128]{3,2,1,0:T(8,128)} %psi.1) | copy-start | bytes 196612

commit v3 on v2

v3 whole, which is shorter than its diff:
```python
import jax
import jax.numpy as jnp
from jax import lax
from jax.experimental import pallas as pl
from jax.experimental.pallas import tpu as pltpu
from jax.sharding import PartitionSpec as P

MESH = pl.DeviceIdType.MESH
HIGH = lax.Precision.HIGHEST
SIZES = (4, 8, 32)
GRID_TOTAL = 4194304
STENCIL = (-205.0 / 72.0, 8.0 / 5.0, -1.0 / 5.0, 8.0 / 315.0, -1.0 / 560.0)
KIN = tuple(-0.5 * c for c in STENCIL)
PAIRS = [(i, j) for j in range(4) for i in range(j + 1)]
HALOS = [(0, 0, 1), (0, 0, -1), (0, 1, 0), (0, -1, 0)]
PLANE = [(0, 0, d) for d in range(1, 32)]
SIDES = (-1, 0, 1)


def here():
    return lax.axis_index("gx"), lax.axis_index("gy"), lax.axis_index("gz")


def at_offset(delta):
    return tuple(
        v if d % n == 0 else (v + (d % n)) & (n - 1) for v, d, n in zip(here(), delta, SIZES)
    )


def lanes(shape):
    return lax.broadcasted_iota(jnp.int32, shape, len(shape) - 1)


def sublanes(shape):
    return lax.broadcasted_iota(jnp.int32, shape, len(shape) - 2)


def row_sum(v):
    total = v[0:8]
    for k in range(8, v.shape[0], 8):
        total = total + v[k : k + 8]
    for shift in (4, 2, 1):
        total = total + pltpu.roll(total, shift, 0)
    return total


def main_kernel(
    orb_hbm, pot_hbm, atom_hbm, points_hbm, count, beta_hbm, coup_hbm,
    image_ref, gram_ref,
    psi, pot, pts, beta, coup, atom,
    zb, hy, pk, xcor, msg, a2, row_own, rows16, onehot, spread,
    r1, pe, xc, kr, stage, row_hub, ba, row_all, xrow,
    lsem, hsend, hrecv, csend, crecv,
):
    f32 = jnp.float32
    loads = [
        pltpu.make_async_copy(orb_hbm, psi, lsem.at[0]),
        pltpu.make_async_copy(points_hbm.at[0, 0, 0], pts, lsem.at[1]),
        pltpu.make_async_copy(beta_hbm.at[0, 0, 0], beta, lsem.at[2]),
        pltpu.make_async_copy(atom_hbm, atom, lsem.at[3]),
        pltpu.make_async_copy(coup_hbm, coup, lsem.at[4]),
        pltpu.make_async_copy(pot_hbm, pot, lsem.at[5]),
    ]
    for load in loads:
        load.start()
    x, y, z = here()
    column = x * 8 + y
    is_hub = column == 0

    def hub_of(d):
        return (0, 0, (z + d) & 31)

    def member(c, d):
        return (c >> 3, c & 7, (z + d) & 31)

    barrier = pltpu.get_barrier_semaphore()

    def greet(device):
        pl.semaphore_signal(barrier, inc=1, device_id=device, device_id_type=MESH)

    for delta in reversed(HALOS):
        greet(at_offset(delta))
    for d in (-1, 1):
        greet(hub_of(d))

    @pl.when(jnp.logical_not(is_hub))
    def _():
        greet(hub_of(0))

    @pl.when(is_hub)
    def _():
        for d in (-1, 1):
            greet(hub_of(d))

        def each(c, carry):
            for d in SIDES:
                greet(member(c, d))
            greet(hub_of(c))
            return carry

        lax.fori_loop(1, 32, each, 0)

    def remote(src, dst, send, recv, device):
        return pltpu.make_async_remote_copy(
            src_ref=src, dst_ref=dst, send_sem=send, recv_sem=recv,
            device_id=device, device_id_type=MESH,
        )

    def wait_bytes(ref, sem):
        pltpu.make_async_copy(ref, ref, sem).wait()

    lane8, sub8 = lanes((8, 128)), sublanes((8, 128))
    loads[0].wait()

    packed = jnp.zeros((8, 128), f32)
    for n in range(4):
        for zz in range(4):
            g = n * 4 + zz
            moved = pltpu.roll(psi[n, zz], (4 + 8 * g) % 128, 1)
            packed = jnp.where(lane8 // 8 == g, moved, packed)
    pk[...] = packed

    pl.semaphore_wait(barrier, jnp.where(is_hub, 4 + 2 + 2 + 31 * 4, 4 + 3))
    halo_copies = [
        (psi, zb.at[0]),
        (psi, zb.at[1]),
        (psi.at[:, :, pl.ds(4, 4)], hy.at[:, :, pl.ds(4, 4)]),
        (psi.at[:, :, pl.ds(0, 4)], hy.at[:, :, pl.ds(0, 4)]),
    ]
    halos = [
        remote(src, dst, hsend.at[k], hrecv.at[k], at_offset(HALOS[k]))
        for k, (src, dst) in enumerate(halo_copies)
    ]
    for halo in halos:
        halo.start()

    @pl.when(jnp.logical_not(is_hub))
    def _():
        remote(pk, pe.at[column], csend.at[4], crecv.at[4], hub_of(0)).start()

    loads[1].wait()
    lo = [pts[8 * h : 8 * h + 8] & 127 for h in range(2)]
    hi = [pts[8 * h : 8 * h + 8] >> 7 for h in range(2)]
    gathered = [[jnp.zeros((8, 128), f32) for _ in range(2)] for _ in range(4)]
    for row in range(32):
        pick = [hi[h] == row for h in range(2)]
        for n in range(4):
            line = jnp.broadcast_to(psi[n, row // 8, row % 8 : row % 8 + 1], (8, 128))
            for h in range(2):
                got = jnp.take_along_axis(line, lo[h], axis=1)
                gathered[n][h] = jnp.where(pick[h], got, gathered[n][h])

    for load in loads[2:]:
        load.wait()
    slots = count[0, 0, 0]
    dir_of, kind_of = [], []
    for b in range(16):
        a = atom[0, 0, 0, b]
        owner = a // 3
        dx = ((owner & 3) - x + 1) & 3
        dy = (((owner >> 2) & 7) - y + 1) & 7
        dz = ((owner >> 5) - z + 1) & 31
        where = jnp.minimum(jnp.maximum(dz * 16 + dy * 3 + dx, 0), 47)
        dir_of.append(where)
        kind_of.append(a - owner * 3)
    dir_lane = jnp.full((48, 128), 63, jnp.int32)
    for b in range(16):
        used = jnp.where(b < slots, dir_of[b], 63)
        dir_lane = jnp.where(lanes((48, 128)) // 8 == b, used, dir_lane)
    select = (sublanes((48, 128)) == dir_lane).astype(f32)

    lane_n, lane_k, lane_p = lane8 // 32, (lane8 // 8) & 3, lane8 & 7
    blocks = []
    for b in range(16):
        block = jnp.zeros((8, 128), f32)
        for n in range(4):
            line = jnp.broadcast_to(gathered[n][b // 8][b % 8 : b % 8 + 1], (8, 128))
            part = jnp.sum(beta[b] * line, axis=1, keepdims=True)
            block = jnp.where(lane_n == n, part, block)
        keep = (lane_p == sub8) & (lane_k == kind_of[b])
        blocks.append(jnp.where(keep, block, 0.0))
    msg[...] = jnp.dot(
        select, jnp.concatenate(blocks, axis=0), precision=HIGH, preferred_element_type=f32
    )

    def send_rows(d):
        src, dst = msg.at[pl.ds(16 * (d + 1), 9)], r1.at[32 * (d + 1) + column, pl.ds(0, 9)]
        remote(src, dst, csend.at[0], crecv.at[0], hub_of(d)).start()

    send_rows(-1)
    send_rows(1)

    @pl.when(jnp.logical_not(is_hub))
    def _():
        send_rows(0)

    li, si = lanes((128, 128)), sublanes((128, 128))
    away = (li - si) & 127
    away = jnp.minimum(away, 128 - away)
    along_x = jnp.where(away == 0, 3.0 * KIN[0], 0.0)
    for o in range(1, 5):
        along_x = jnp.where(away == o, KIN[o], along_x)
    flat = psi[...].reshape(128, 128)
    base = jnp.dot(flat, along_x, precision=HIGH, preferred_element_type=f32)

    for b in range(16):
        line = jnp.broadcast_to(lo[b // 8][b % 8 : b % 8 + 1], (128, 128))
        onehot[:, pl.ds(b * 128, 128)] = (si == line).astype(jnp.bfloat16)

    for halo in halos:
        halo.wait_recv()
    sums = [None] * len(PAIRS)
    for zz in range(4):
        image = []
        for n in range(4):
            own, other = psi[n, zz], hy[n, zz]
            total = base[(n * 4 + zz) * 8 : (n * 4 + zz) * 8 + 8]
            for o in range(1, 5):
                up = psi[n, zz + o] if zz + o < 4 else zb[1, n, zz + o - 4]
                down = psi[n, zz - o] if zz - o >= 0 else zb[0, n, zz - o + 4]
                before = pltpu.roll(jnp.where(sub8 < 8 - o, own, other), o, 0)
                after = pltpu.roll(jnp.where(sub8 >= o, own, other), 8 - o, 0)
                total = total + KIN[o] * ((up + down) + (before + after))
            total = total + pot[zz] * own
            image.append(total)
            image_ref[n, zz] = total
        for k, (i, j) in enumerate(PAIRS):
            term = psi[i, zz] * image[j]
            sums[k] = term if sums[k] is None else sums[k] + term
    local = jnp.zeros((8, 128), f32)
    for k, (i, j) in enumerate(PAIRS):
        total = jnp.sum(sums[k], axis=1, keepdims=True)
        local = jnp.where(lane8 == j * 32 + (j - i) * 8, total, local)
    row_own[...] = row_sum(local)

    @pl.when(jnp.logical_not(is_hub))
    def _():
        remote(
            row_own.at[pl.ds(0, 1)], kr.at[column, pl.ds(0, 1)], csend.at[5], crecv.at[5], hub_of(0)
        ).start()

    @pl.when(is_hub)
    def _():
        kr[0] = row_own[...]
        pe[0] = pk[...]
        r1[32, pl.ds(0, 9)] = msg[pl.ds(16, 9)]
        sj, lj = si & 7, li & 7
        edge = jnp.zeros((128, 128), f32)
        for o in range(1, 5):
            left = (sj < 4) & (lj >= 4) & (lj - sj == o)
            right = (sj >= 4) & (lj < 4) & (sj - lj == o)
            edge = jnp.where((si // 8 == li // 8) & (left | right), KIN[o], edge)
        tiles = []
        for c in range(2):
            tile = jnp.concatenate([coup[c], jnp.zeros((8, 120), f32)], axis=1)
            for shift in (8, 16, 32, 64):
                tile = tile + pltpu.roll(tile, shift, 1)
            tiles.append(tile)
        couple = jnp.concatenate(
            [jnp.where(lane8 // 8 == r, tiles[0 if r % 4 == 0 else 1], 0.0) for r in range(16)],
            axis=0,
        )

        def reaches(box, c, r):
            third = (r * 11) >> 5
            tx = ((c >> 3) + (r - 3 * third) + 3) & 3
            ty = ((c & 7) + third + 7) & 7
            return ((r < 9) & (box == tx * 8 + ty)).astype(f32)

        col, box = lanes((32, 512)), sublanes((32, 512))
        collect = reaches(box, col >> 4, col & 15)
        row, box = sublanes((512, 32)), lanes((512, 32))
        spread_out = reaches(box, row >> 4, row & 15)

        wait_bytes(pe.at[pl.ds(0, 31)], crecv.at[4])
        edges = []
        for c in range(32):
            before, after = (c + 24) % 32, (c + 8) % 32
            edges.append(jnp.where(lane8 & 7 < 4, pe[before], pe[after]) - pe[c])
        change = jnp.dot(
            jnp.concatenate(edges, axis=0), edge, precision=HIGH, preferred_element_type=f32
        )
        outer = [jnp.zeros((8, 128), f32) for _ in range(4)]
        for c in range(32):
            part = change[8 * c : 8 * c + 8]
            xc[c] = part
            for s in range(4):
                outer[s] = outer[s] + (pltpu.roll(pe[c], 32 * s, 1) if s else pe[c]) * part

        wait_bytes(r1.at[pl.ds(0, 95), pl.ds(0, 9)], crecv.at[0])
        gathered_rows = (r1[pl.ds(0, 32)] + r1[pl.ds(64, 32)]) + r1[pl.ds(32, 32)]
        gathered_rows = jnp.where(sublanes((32, 16, 128)) < 9, gathered_rows, 0.0)
        coef = jnp.dot(
            collect, gathered_rows.reshape(512, 128), precision=HIGH, preferred_element_type=f32
        )
        applied = jnp.dot(coef, couple, precision=HIGH, preferred_element_type=f32)
        stage[...] = jnp.dot(
            spread_out, applied, precision=HIGH, preferred_element_type=f32
        ).reshape(32, 16, 128)

        def hand_out(c, d):
            remote(
                stage.at[c, pl.ds(0, 9)], a2.at[pl.ds(16 * (1 - d), 9)], csend.at[1], crecv.at[1],
                member(c, d),
            ).start()

        def each(c, carry):
            for d in SIDES:
                hand_out(c, d)
            remote(xc.at[c], xcor, csend.at[6], crecv.at[6], member(c, 0)).start()
            return carry

        hand_out(0, -1)
        hand_out(0, 1)
        lax.fori_loop(1, 32, each, 0)
        a2[pl.ds(16, 9)] = stage[0, pl.ds(0, 9)]
        xcor[...] = xc[0]

        for v in range(4):
            c8, a8 = coef[8 * v : 8 * v + 8], applied[8 * v : 8 * v + 8]
            for s in range(4):
                outer[s] = outer[s] + (pltpu.roll(c8, 32 * s, 1) if s else c8) * a8
        placed = jnp.zeros((8, 128), f32)
        for s in range(4):
            part = outer[s]
            part = (part + pltpu.roll(part, 120, 1)) + (pltpu.roll(part, 112, 1) + pltpu.roll(part, 104, 1))
            part = jnp.where(lane8 & 31 < 8, part, 0.0)
            placed = placed + (pltpu.roll(part, 8 * s, 1) if s else part)
        placed = row_sum(placed)
        wait_bytes(kr.at[pl.ds(0, 31), pl.ds(0, 1)], crecv.at[5])
        kinetic = kr[0]
        for c in range(1, 32):
            kinetic = kinetic + kr[c]
        row_hub[...] = placed + kinetic
        ba[pl.ds(31, 1)] = row_hub[pl.ds(0, 1)]
        for k, delta in enumerate(PLANE):
            remote(
                row_hub.at[pl.ds(0, 1)], ba.at[pl.ds(k, 1)], csend.at[2], crecv.at[2], at_offset(delta)
            ).start()

    @pl.when(is_hub)
    def _():
        wait_bytes(a2.at[pl.ds(0, 18)], crecv.at[1])

    @pl.when(jnp.logical_not(is_hub))
    def _():
        wait_bytes(a2.at[pl.ds(0, 27)], crecv.at[1])
        wait_bytes(xcor, crecv.at[6])

    for b in range(16):
        rows16[pl.ds(b, 1)] = a2[pl.ds(dir_of[b], 1)]
    spots = []
    for h in range(2):
        kind = jnp.zeros((8, 128), jnp.int32)
        for b in range(8):
            kind = jnp.where(sub8 == b, kind_of[h * 8 + b], kind)
        spots.append(kind * 8 + lane_p)
    left = []
    for n in range(4):
        for h in range(2):
            got = jnp.take_along_axis(rows16[pl.ds(h * 8, 8)], spots[h] + 32 * n, axis=1)
            slot = sub8 + 8 * h
            left.append(jnp.where((lane8 // 8 == slot) & (slot < slots), got, 0.0))
    values = jnp.dot(
        jnp.concatenate(left, axis=0), beta[...].reshape(128, 128), precision=HIGH,
        preferred_element_type=f32,
    )
    high = values.astype(jnp.bfloat16).astype(f32)
    low = values - high
    for b in range(16):
        line = jnp.broadcast_to(hi[b // 8][b % 8 : b % 8 + 1], (32, 128))
        pick = sublanes((32, 128)) == line
        for part, source in enumerate((high, low)):
            for n in range(4):
                r = n * 16 + b
                piece = jnp.where(pick, jnp.broadcast_to(source[r : r + 1], (32, 128)), 0.0)
                spread[pl.ds(part * 128 + n * 32, 32), pl.ds(b * 128, 128)] = piece.astype(jnp.bfloat16)
    grid = lax.dot_general(
        spread[...], onehot[...], (((1,), (1,)), ((), ())), preferred_element_type=f32
    )
    at_edge = (lane8 < 4) | (lane8 >= 124)
    for n in range(4):
        for zz in range(4):
            g = n * 4 + zz
            moved = pltpu.roll(xcor[...], (124 - 8 * g) % 128, 1)
            projected = grid[8 * g : 8 * g + 8] + grid[128 + 8 * g : 136 + 8 * g]
            image_ref[n, zz] = image_ref[n, zz] + jnp.where(at_edge, moved, 0.0) + projected

    @pl.when(is_hub)
    def _():
        wait_bytes(ba.at[pl.ds(0, 31)], crecv.at[2])
        row_all[...] = row_sum(ba[...])

        def each(c, carry):
            row = row_all.at[pl.ds(0, 1)]
            remote(row, xrow.at[pl.ds(0, 1)], csend.at[3], crecv.at[3], member(c, 0)).start()
            return carry

        lax.fori_loop(1, 32, each, 0)
        gram_ref[...] = row_all[...]
        wait_bytes(msg.at[pl.ds(0, 18)], csend.at[0])
        wait_bytes(r1.at[pl.ds(0, 95), pl.ds(0, 9)], csend.at[1])
        wait_bytes(pe.at[pl.ds(0, 31)], csend.at[6])
        wait_bytes(ba.at[pl.ds(0, 31)], csend.at[2])
        wait_bytes(kr.at[pl.ds(0, 31), pl.ds(0, 1)], csend.at[3])

    @pl.when(jnp.logical_not(is_hub))
    def _():
        wait_bytes(xrow.at[pl.ds(0, 1)], crecv.at[3])
        gram_ref[...] = jnp.broadcast_to(xrow[pl.ds(0, 1)], (8, 128))
        wait_bytes(msg.at[pl.ds(0, 27)], csend.at[0])
        wait_bytes(pk, csend.at[4])
        wait_bytes(row_own.at[pl.ds(0, 1)], csend.at[5])

    for halo in halos:
        halo.wait_send()


def residual_kernel(psi, image, gram, image_out, residual_out, residual, sem):
    copies = [pltpu.make_async_copy(image, image_out, sem.at[4])]
    copies[0].start()
    lane8 = lanes((8, 128))
    row = gram[...]
    weight = {}
    for i, j in PAIRS:
        group = j * 4 + (j - i)
        total = jnp.sum(jnp.where(lane8 // 8 == group, row, 0.0), axis=1, keepdims=True)
        total = jnp.broadcast_to(total, (8, 128)) * (1.0 / GRID_TOTAL)
        weight[i, j] = weight[j, i] = total
    for j in range(4):
        for z in range(4):
            total = image[j, z]
            for i in range(4):
                total = total - weight[i, j] * psi[i, z]
            residual[j, z] = total
        copies.append(pltpu.make_async_copy(residual.at[j], residual_out.at[j], sem.at[j]))
        copies[-1].start()
    for copy in copies:
        copy.wait()


def on_device(orbitals, potential, block_atom, block_points, block_count, projector_values, coupling):
    f32, i32 = jnp.float32, jnp.int32
    hbm = pl.BlockSpec(memory_space=pl.ANY)
    vmem = pl.BlockSpec(memory_space=pltpu.VMEM)
    field = jax.ShapeDtypeStruct((4, 4, 8, 128), f32)
    held = [
        pltpu.with_memory_space_constraint(v, pltpu.HBM)
        for v in (orbitals, potential, block_atom, block_points, projector_values, coupling)
    ]
    held.insert(4, block_count)
    image, gram = pl.pallas_call(
        main_kernel,
        out_shape=(pltpu.VMEM((4, 4, 8, 128), f32), pltpu.VMEM((8, 128), f32)),
        in_specs=[hbm] * 4 + [pl.BlockSpec(memory_space=pltpu.SMEM)] + [hbm] * 2,
        out_specs=(vmem, vmem),
        scratch_shapes=[
            pltpu.VMEM((4, 4, 8, 128), f32),
            pltpu.VMEM((4, 8, 128), f32),
            pltpu.VMEM((16, 128), i32),
            pltpu.VMEM((16, 8, 128), f32),
            pltpu.VMEM((2, 8, 8), f32),
            pltpu.SMEM((1, 1, 1, 16), i32),
            pltpu.VMEM((2, 4, 4, 8, 128), f32),
            pltpu.VMEM((4, 4, 8, 128), f32),
            pltpu.VMEM((8, 128), f32),
            pltpu.VMEM((8, 128), f32),
            pltpu.VMEM((48, 128), f32),
            pltpu.VMEM((48, 128), f32),
            pltpu.VMEM((8, 128), f32),
            pltpu.VMEM((16, 128), f32),
            pltpu.VMEM((128, 2048), jnp.bfloat16),
            pltpu.VMEM((256, 2048), jnp.bfloat16),
            pltpu.VMEM((96, 16, 128), f32),
            pltpu.VMEM((32, 8, 128), f32),
            pltpu.VMEM((32, 8, 128), f32),
            pltpu.VMEM((32, 8, 128), f32),
            pltpu.VMEM((32, 16, 128), f32),
            pltpu.VMEM((8, 128), f32),
            pltpu.VMEM((32, 128), f32),
            pltpu.VMEM((8, 128), f32),
            pltpu.VMEM((8, 128), f32),
            pltpu.SemaphoreType.DMA((6,)),
            pltpu.SemaphoreType.DMA((4,)),
            pltpu.SemaphoreType.DMA((4,)),
            pltpu.SemaphoreType.DMA((7,)),
            pltpu.SemaphoreType.DMA((7,)),
        ],
        compiler_params=pltpu.CompilerParams(
            collective_id=0, has_side_effects=True, vmem_limit_bytes=24 * 1024 * 1024
        ),
    )(*held)
    return pl.pallas_call(
        residual_kernel,
        out_shape=(field, field),
        in_specs=[vmem] * 3,
        out_specs=(hbm, hbm),
        scratch_shapes=[pltpu.VMEM((4, 4, 8, 128), f32), pltpu.SemaphoreType.DMA((5,))],
        compiler_params=pltpu.CompilerParams(vmem_limit_bytes=16 * 1024 * 1024),
    )(orbitals, image, gram)


def solution(mesh):
    return jax.shard_map(
        on_device,
        mesh=mesh,
        in_specs=(
            P(None, "gz", "gy", "gx"),
            P("gz", "gy", "gx"),
            P("gz", "gy", "gx", None),
            P("gz", "gy", "gx", None, None),
            P("gz", "gy", "gx"),
            P("gz", "gy", "gx", None, None, None),
            P(),
        ),
        out_specs=(P(None, "gz", "gy", "gx"), P(None, "gz", "gy", "gx")),
        check_vma=False,
    )
```

time: 46.5 us -> 41.5 us (0.89)
  Pallas kernels: 45 us -> 40 us
    pallas_call x1, Pallas kernels: 44.2 us -> 39.2 us  [on_device(): pl.pallas_call(main_kernel, out_shape=(pltpu.VMEM((4, 4, 8, 128), f32), p...]
where the time goes in v3:
time: 41.5 us; the launch traced here: 41.3 us
  Pallas kernels  40 us (96%)
  between operations  1.3 us (3%)
    pallas_call x1, Pallas kernels, on_device(): pl.pallas_call(main_kernel, out_shape=(pltpu.VMEM((4, 4, 8, 128), f32), p...  39.2 us

profile of v3, /device:TPU:1, one launch (start us, length us, event | category | flops | bytes accessed | tf_op | source)
XLA Modules:
  0.0 41.3 jit_solution(11156325340712092234)
XLA Ops:
  1.3 0.0 copy-start
  1.3 39.2 %shard_map.86 = (f32[4,4,8,128]{3,2,1,0:T(8,128)S(1)}, f32[8,128]{1,0:T(8,128)S(1)}) custom-call(f32[4,4,8,128]{3,2,1,0:T(8,128)} %psi.1, f32[4,8,128]{2,1,0:T(8,128)} %pot_hbm.1, s32[1,1,1,16]{3,2,1,0:T(1,128)} %atom_hbm.1, s32[1,1,1,16,128]{4,3,2,1,0:T(8,128)} %points_hbm.1, s32[1,1,1]{2,1,0:T(1,128)S(6)} %copy.9.count, ...), custom_call_target="tpu_custom_call" | custom-call | tf_op jit(solution)/shard_map/pallas_call | solution.py:452
  40.5 0.0 copy-done
  40.5 0.8 %shard_map.87 = (f32[4,4,8,128]{3,2,1,0:T(8,128)}, f32[4,4,8,128]{3,2,1,0:T(8,128)}) custom-call(f32[4,4,8,128]{3,2,1,0:T(8,128)S(1)} %copy-done, f32[4,4,8,128]{3,2,1,0:T(8,128)S(1)} %get-tuple-element.4.image, f32[8,128]{1,0:T(8,128)S(1)} %get-tuple-element.5.gram), custom_call_target="tpu_custom_call" | custom-call | tf_op jit(solution)/shard_map/pallas_call | solution.py:493
Async XLA Ops:
  1.3 39.2 %copy-start = (f32[4,4,8,128]{3,2,1,0:T(8,128)S(1)}, f32[4,4,8,128]{3,2,1,0:T(8,128)}, u32[]{:S(2)}) copy-start(f32[4,4,8,128]{3,2,1,0:T(8,128)} %psi.1) | copy-start | bytes 196612

commit v4 on v3

--- a/solution.py
+++ b/solution.py
@@ -13,8 +13,13 @@
 KIN = tuple(-0.5 * c for c in STENCIL)
 PAIRS = [(i, j) for j in range(4) for i in range(j + 1)]
 HALOS = [(0, 0, 1), (0, 0, -1), (0, 1, 0), (0, -1, 0)]
-PLANE = [(0, 0, d) for d in range(1, 32)]
+PLANE = sorted(
+    [(0, 0, d) for d in range(1, 32)],
+    key=lambda delta: -min(delta[2] % 8, 8 - delta[2] % 8) - min(delta[2] // 8, 4 - delta[2] // 8),
+)
 SIDES = (-1, 0, 1)
+HUB = 1
+MEMBERS = [c for c in range(32) if c != HUB]
 
 
 def here():
@@ -65,10 +70,10 @@
         load.start()
     x, y, z = here()
     column = x * 8 + y
-    is_hub = column == 0
+    is_hub = column == HUB
 
     def hub_of(d):
-        return (0, 0, (z + d) & 31)
+        return (0, HUB, (z + d) & 31)
 
     def member(c, d):
         return (c >> 3, c & 7, (z + d) & 31)
@@ -92,13 +97,11 @@
         for d in (-1, 1):
             greet(hub_of(d))
 
-        def each(c, carry):
+        for c in MEMBERS:
             for d in SIDES:
                 greet(member(c, d))
-            greet(hub_of(c))
-            return carry
-
-        lax.fori_loop(1, 32, each, 0)
+        for d in range(1, 32):
+            greet(hub_of(d))
 
     def remote(src, dst, send, recv, device):
         return pltpu.make_async_remote_copy(
@@ -241,9 +244,9 @@
 
     @pl.when(is_hub)
     def _():
-        kr[0] = row_own[...]
-        pe[0] = pk[...]
-        r1[32, pl.ds(0, 9)] = msg[pl.ds(16, 9)]
+        kr[HUB] = row_own[...]
+        pe[HUB] = pk[...]
+        r1[32 + HUB, pl.ds(0, 9)] = msg[pl.ds(16, 9)]
         sj, lj = si & 7, li & 7
         edge = jnp.zeros((128, 128), f32)
         for o in range(1, 5):
@@ -294,27 +297,12 @@
             collect, gathered_rows.reshape(512, 128), precision=HIGH, preferred_element_type=f32
         )
         applied = jnp.dot(coef, couple, precision=HIGH, preferred_element_type=f32)
-        stage[...] = jnp.dot(
-            spread_out, applied, precision=HIGH, preferred_element_type=f32
-        ).reshape(32, 16, 128)
 
         def hand_out(c, d):
             remote(
                 stage.at[c, pl.ds(0, 9)], a2.at[pl.ds(16 * (1 - d), 9)], csend.at[1], crecv.at[1],
                 member(c, d),
             ).start()
-
-        def each(c, carry):
-            for d in SIDES:
-                hand_out(c, d)
-            remote(xc.at[c], xcor, csend.at[6], crecv.at[6], member(c, 0)).start()
-            return carry
-
-        hand_out(0, -1)
-        hand_out(0, 1)
-        lax.fori_loop(1, 32, each, 0)
-        a2[pl.ds(16, 9)] = stage[0, pl.ds(0, 9)]
-        xcor[...] = xc[0]
 
         for v in range(4):
             c8, a8 = coef[8 * v : 8 * v + 8], applied[8 * v : 8 * v + 8]
@@ -337,6 +325,17 @@
             remote(
                 row_hub.at[pl.ds(0, 1)], ba.at[pl.ds(k, 1)], csend.at[2], crecv.at[2], at_offset(delta)
             ).start()
+        stage[...] = jnp.dot(
+            spread_out, applied, precision=HIGH, preferred_element_type=f32
+        ).reshape(32, 16, 128)
+        hand_out(HUB, -1)
+        hand_out(HUB, 1)
+        for c in MEMBERS:
+            for d in SIDES:
+                hand_out(c, d)
+            remote(xc.at[c], xcor, csend.at[6], crecv.at[6], member(c, 0)).start()
+        a2[pl.ds(16, 9)] = stage[HUB, pl.ds(0, 9)]
+        xcor[...] = xc[HUB]
 
     @pl.when(is_hub)
     def _():
@@ -391,12 +390,9 @@
         wait_bytes(ba.at[pl.ds(0, 31)], crecv.at[2])
         row_all[...] = row_sum(ba[...])
 
-        def each(c, carry):
+        for c in MEMBERS:
             row = row_all.at[pl.ds(0, 1)]
             remote(row, xrow.at[pl.ds(0, 1)], csend.at[3], crecv.at[3], member(c, 0)).start()
-            return carry
-
-        lax.fori_loop(1, 32, each, 0)
         gram_ref[...] = row_all[...]
         wait_bytes(msg.at[pl.ds(0, 18)], csend.at[0])
         wait_bytes(r1.at[pl.ds(0, 95), pl.ds(0, 9)], csend.at[1])

time: 41.5 us -> 39.6 us (0.954)
  Pallas kernels: 40 us -> 38.1 us
    pallas_call x1, Pallas kernels: 39.2 us -> 37.3 us  [on_device(): pl.pallas_call(main_kernel, out_shape=(pltpu.VMEM((4, 4, 8, 128), f32), p...]
where the time goes in v4:
time: 39.6 us; the launch traced here: 39.4 us
  Pallas kernels  38.1 us (96%)
  between operations  1.3 us (3%)
    pallas_call x1, Pallas kernels, on_device(): pl.pallas_call(main_kernel, out_shape=(pltpu.VMEM((4, 4, 8, 128), f32), p...  37.3 us

profile of v4, /device:TPU:1, one launch (start us, length us, event | category | flops | bytes accessed | tf_op | source)
XLA Modules:
  0.0 39.4 jit_solution(11500660755224214135)
XLA Ops:
  1.3 0.0 copy-start
  1.3 37.3 %shard_map.86 = (f32[4,4,8,128]{3,2,1,0:T(8,128)S(1)}, f32[8,128]{1,0:T(8,128)S(1)}) custom-call(f32[4,4,8,128]{3,2,1,0:T(8,128)} %psi.1, f32[4,8,128]{2,1,0:T(8,128)} %pot_hbm.1, s32[1,1,1,16]{3,2,1,0:T(1,128)} %atom_hbm.1, s32[1,1,1,16,128]{4,3,2,1,0:T(8,128)} %points_hbm.1, s32[1,1,1]{2,1,0:T(1,128)S(6)} %copy.9.count, ...), custom_call_target="tpu_custom_call" | custom-call | tf_op jit(solution)/shard_map/pallas_call | solution.py:448
  38.6 0.0 copy-done
  38.6 0.8 %shard_map.87 = (f32[4,4,8,128]{3,2,1,0:T(8,128)}, f32[4,4,8,128]{3,2,1,0:T(8,128)}) custom-call(f32[4,4,8,128]{3,2,1,0:T(8,128)S(1)} %copy-done, f32[4,4,8,128]{3,2,1,0:T(8,128)S(1)} %get-tuple-element.4.image, f32[8,128]{1,0:T(8,128)S(1)} %get-tuple-element.5.gram), custom_call_target="tpu_custom_call" | custom-call | tf_op jit(solution)/shard_map/pallas_call | solution.py:489
Async XLA Ops:
  1.3 37.3 %copy-start = (f32[4,4,8,128]{3,2,1,0:T(8,128)S(1)}, f32[4,4,8,128]{3,2,1,0:T(8,128)}, u32[]{:S(2)}) copy-start(f32[4,4,8,128]{3,2,1,0:T(8,128)} %psi.1) | copy-start | bytes 196612

commit v5 on v4

--- a/solution.py
+++ b/solution.py
@@ -12,7 +12,8 @@
 STENCIL = (-205.0 / 72.0, 8.0 / 5.0, -1.0 / 5.0, 8.0 / 315.0, -1.0 / 560.0)
 KIN = tuple(-0.5 * c for c in STENCIL)
 PAIRS = [(i, j) for j in range(4) for i in range(j + 1)]
-HALOS = [(0, 0, 1), (0, 0, -1), (0, 1, 0), (0, -1, 0)]
+UP, DOWN = (0, 0, 1), (0, 0, -1)
+HALOS = [UP, DOWN, (0, 1, 0), (0, -1, 0), UP, DOWN]
 PLANE = sorted(
     [(0, 0, d) for d in range(1, 32)],
     key=lambda delta: -min(delta[2] % 8, 8 - delta[2] % 8) - min(delta[2] // 8, 4 - delta[2] // 8),
@@ -53,8 +54,8 @@
     orb_hbm, pot_hbm, atom_hbm, points_hbm, count, beta_hbm, coup_hbm,
     image_ref, gram_ref,
     psi, pot, pts, beta, coup, atom,
-    zb, hy, pk, xcor, msg, a2, row_own, rows16, onehot, spread,
-    r1, pe, xc, kr, stage, row_hub, ba, row_all, xrow,
+    zb, hy, pk, msg, a2, row_own, rows16, onehot, spread,
+    r1, pe, kr, stage, row_hub, ba, row_all, xrow, sent,
     lsem, hsend, hrecv, csend, crecv,
 ):
     f32 = jnp.float32
@@ -83,7 +84,7 @@
     def greet(device):
         pl.semaphore_signal(barrier, inc=1, device_id=device, device_id_type=MESH)
 
-    for delta in reversed(HALOS):
+    for delta in reversed(HALOS[:4]):
         greet(at_offset(delta))
     for d in (-1, 1):
         greet(hub_of(d))
@@ -125,16 +126,18 @@
 
     pl.semaphore_wait(barrier, jnp.where(is_hub, 4 + 2 + 2 + 31 * 4, 4 + 3))
     halo_copies = [
-        (psi, zb.at[0]),
-        (psi, zb.at[1]),
+        (psi.at[:, pl.ds(2, 2)], zb.at[0, :, pl.ds(2, 2)]),
+        (psi.at[:, pl.ds(0, 2)], zb.at[1, :, pl.ds(0, 2)]),
         (psi.at[:, :, pl.ds(4, 4)], hy.at[:, :, pl.ds(4, 4)]),
         (psi.at[:, :, pl.ds(0, 4)], hy.at[:, :, pl.ds(0, 4)]),
+        (psi.at[:, pl.ds(0, 2)], zb.at[0, :, pl.ds(0, 2)]),
+        (psi.at[:, pl.ds(2, 2)], zb.at[1, :, pl.ds(2, 2)]),
     ]
     halos = [
         remote(src, dst, hsend.at[k], hrecv.at[k], at_offset(HALOS[k]))
         for k, (src, dst) in enumerate(halo_copies)
     ]
-    for halo in halos:
+    for halo in halos[:4]:
         halo.start()
 
     @pl.when(jnp.logical_not(is_hub))
@@ -156,7 +159,7 @@
     for load in loads[2:]:
         load.wait()
     slots = count[0, 0, 0]
-    dir_of, kind_of = [], []
+    dir_of, back_of, kind_of = [], [], []
     for b in range(16):
         a = atom[0, 0, 0, b]
         owner = a // 3
@@ -164,7 +167,9 @@
         dy = (((owner >> 2) & 7) - y + 1) & 7
         dz = ((owner >> 5) - z + 1) & 31
         where = jnp.minimum(jnp.maximum(dz * 16 + dy * 3 + dx, 0), 47)
+        back = jnp.minimum(jnp.maximum(dz * 24 + dy * 3 + dx + 8, 0), 71)
         dir_of.append(where)
+        back_of.append(back)
         kind_of.append(a - owner * 3)
     dir_lane = jnp.full((48, 128), 63, jnp.int32)
     for b in range(16):
@@ -197,6 +202,9 @@
     def _():
         send_rows(0)
 
+    for halo in halos[4:]:
+        halo.start()
+
     li, si = lanes((128, 128)), sublanes((128, 128))
     away = (li - si) & 127
     away = jnp.minimum(away, 128 - away)
@@ -210,8 +218,8 @@
         line = jnp.broadcast_to(lo[b // 8][b % 8 : b % 8 + 1], (128, 128))
         onehot[:, pl.ds(b * 128, 128)] = (si == line).astype(jnp.bfloat16)
 
-    for halo in halos:
-        halo.wait_recv()
+    halos[2].wait_recv()
+    halos[3].wait_recv()
     sums = [None] * len(PAIRS)
     for zz in range(4):
         image = []
@@ -219,17 +227,34 @@
             own, other = psi[n, zz], hy[n, zz]
             total = base[(n * 4 + zz) * 8 : (n * 4 + zz) * 8 + 8]
             for o in range(1, 5):
-                up = psi[n, zz + o] if zz + o < 4 else zb[1, n, zz + o - 4]
-                down = psi[n, zz - o] if zz - o >= 0 else zb[0, n, zz - o + 4]
                 before = pltpu.roll(jnp.where(sub8 < 8 - o, own, other), o, 0)
                 after = pltpu.roll(jnp.where(sub8 >= o, own, other), 8 - o, 0)
-                total = total + KIN[o] * ((up + down) + (before + after))
+                near = before + after
+                if zz + o < 4:
+                    near = near + psi[n, zz + o]
+                if zz - o >= 0:
+                    near = near + psi[n, zz - o]
+                total = total + KIN[o] * near
             total = total + pot[zz] * own
             image.append(total)
             image_ref[n, zz] = total
         for k, (i, j) in enumerate(PAIRS):
             term = psi[i, zz] * image[j]
             sums[k] = term if sums[k] is None else sums[k] + term
+    halos[0].wait_recv()
+    halos[1].wait_recv()
+    for zz in range(4):
+        cross = []
+        for n in range(4):
+            total = KIN[4 - zz] * zb[1, n, 0]
+            if zz >= 1:
+                total = total + KIN[5 - zz] * zb[1, n, 1]
+            for layer in (2, 3):
+                if zz >= 2 and layer >= zz:
+                    total = total + KIN[4 + zz - layer] * zb[0, n, layer]
+            cross.append(total)
+        for k, (i, j) in enumerate(PAIRS):
+            sums[k] = sums[k] + (psi[i, zz] * cross[j] + psi[j, zz] * cross[i])
     local = jnp.zeros((8, 128), f32)
     for k, (i, j) in enumerate(PAIRS):
         total = jnp.sum(sums[k], axis=1, keepdims=True)
@@ -286,7 +311,7 @@
         outer = [jnp.zeros((8, 128), f32) for _ in range(4)]
         for c in range(32):
             part = change[8 * c : 8 * c + 8]
-            xc[c] = part
+            stage[c, pl.ds(0, 8)] = part
             for s in range(4):
                 outer[s] = outer[s] + (pltpu.roll(pe[c], 32 * s, 1) if s else pe[c]) * part
 
@@ -298,12 +323,20 @@
         )
         applied = jnp.dot(coef, couple, precision=HIGH, preferred_element_type=f32)
 
+        stage[:, pl.ds(8, 16)] = jnp.dot(
+            spread_out, applied, precision=HIGH, preferred_element_type=f32
+        ).reshape(32, 16, 128)
+
         def hand_out(c, d):
+            first, rows = (0, 17) if d == 0 else (8, 9)
             remote(
-                stage.at[c, pl.ds(0, 9)], a2.at[pl.ds(16 * (1 - d), 9)], csend.at[1], crecv.at[1],
-                member(c, d),
+                stage.at[c, pl.ds(first, rows)], a2.at[pl.ds(24 * (1 - d) + first, rows)],
+                csend.at[1], crecv.at[1], member(c, d),
             ).start()
 
+        hand_out(HUB, -1)
+        hand_out(HUB, 1)
+        a2[pl.ds(24, 17)] = stage[HUB, pl.ds(0, 17)]
         for v in range(4):
             c8, a8 = coef[8 * v : 8 * v + 8], applied[8 * v : 8 * v + 8]
             for s in range(4):
@@ -325,17 +358,9 @@
             remote(
                 row_hub.at[pl.ds(0, 1)], ba.at[pl.ds(k, 1)], csend.at[2], crecv.at[2], at_offset(delta)
             ).start()
-        stage[...] = jnp.dot(
-            spread_out, applied, precision=HIGH, preferred_element_type=f32
-        ).reshape(32, 16, 128)
-        hand_out(HUB, -1)
-        hand_out(HUB, 1)
         for c in MEMBERS:
             for d in SIDES:
                 hand_out(c, d)
-            remote(xc.at[c], xcor, csend.at[6], crecv.at[6], member(c, 0)).start()
-        a2[pl.ds(16, 9)] = stage[HUB, pl.ds(0, 9)]
-        xcor[...] = xc[HUB]
 
     @pl.when(is_hub)
     def _():
@@ -343,11 +368,12 @@
 
     @pl.when(jnp.logical_not(is_hub))
     def _():
-        wait_bytes(a2.at[pl.ds(0, 27)], crecv.at[1])
-        wait_bytes(xcor, crecv.at[6])
-
+        wait_bytes(a2.at[pl.ds(0, 35)], crecv.at[1])
+
+    halos[4].wait_recv()
+    halos[5].wait_recv()
     for b in range(16):
-        rows16[pl.ds(b, 1)] = a2[pl.ds(dir_of[b], 1)]
+        rows16[pl.ds(b, 1)] = a2[pl.ds(back_of[b], 1)]
     spots = []
     for h in range(2):
         kind = jnp.zeros((8, 128), jnp.int32)
@@ -381,9 +407,15 @@
     for n in range(4):
         for zz in range(4):
             g = n * 4 + zz
-            moved = pltpu.roll(xcor[...], (124 - 8 * g) % 128, 1)
+            moved = pltpu.roll(a2[pl.ds(24, 8)], (124 - 8 * g) % 128, 1)
             projected = grid[8 * g : 8 * g + 8] + grid[128 + 8 * g : 136 + 8 * g]
-            image_ref[n, zz] = image_ref[n, zz] + jnp.where(at_edge, moved, 0.0) + projected
+            total = image_ref[n, zz] + jnp.where(at_edge, moved, 0.0)
+            for o in range(1, 5):
+                if zz + o >= 4:
+                    total = total + KIN[o] * zb[1, n, zz + o - 4]
+                if zz - o < 0:
+                    total = total + KIN[o] * zb[0, n, zz - o + 4]
+            image_ref[n, zz] = total + projected
 
     @pl.when(is_hub)
     def _():
@@ -395,8 +427,7 @@
             remote(row, xrow.at[pl.ds(0, 1)], csend.at[3], crecv.at[3], member(c, 0)).start()
         gram_ref[...] = row_all[...]
         wait_bytes(msg.at[pl.ds(0, 18)], csend.at[0])
-        wait_bytes(r1.at[pl.ds(0, 95), pl.ds(0, 9)], csend.at[1])
-        wait_bytes(pe.at[pl.ds(0, 31)], csend.at[6])
+        wait_bytes(sent.at[pl.ds(0, 95 * 9 + 31 * 8)], csend.at[1])
         wait_bytes(ba.at[pl.ds(0, 31)], csend.at[2])
         wait_bytes(kr.at[pl.ds(0, 31), pl.ds(0, 1)], csend.at[3])
 
@@ -460,9 +491,8 @@
             pltpu.VMEM((2, 4, 4, 8, 128), f32),
             pltpu.VMEM((4, 4, 8, 128), f32),
             pltpu.VMEM((8, 128), f32),
-            pltpu.VMEM((8, 128), f32),
             pltpu.VMEM((48, 128), f32),
-            pltpu.VMEM((48, 128), f32),
+            pltpu.VMEM((72, 128), f32),
             pltpu.VMEM((8, 128), f32),
             pltpu.VMEM((16, 128), f32),
             pltpu.VMEM((128, 2048), jnp.bfloat16),
@@ -470,17 +500,17 @@
             pltpu.VMEM((96, 16, 128), f32),
             pltpu.VMEM((32, 8, 128), f32),
             pltpu.VMEM((32, 8, 128), f32),
-            pltpu.VMEM((32, 8, 128), f32),
-            pltpu.VMEM((32, 16, 128), f32),
+            pltpu.VMEM((32, 24, 128), f32),
             pltpu.VMEM((8, 128), f32),
             pltpu.VMEM((32, 128), f32),
             pltpu.VMEM((8, 128), f32),
             pltpu.VMEM((8, 128), f32),
+            pltpu.VMEM((1104, 128), f32),
             pltpu.SemaphoreType.DMA((6,)),
-            pltpu.SemaphoreType.DMA((4,)),
-            pltpu.SemaphoreType.DMA((4,)),
-            pltpu.SemaphoreType.DMA((7,)),
-            pltpu.SemaphoreType.DMA((7,)),
+            pltpu.SemaphoreType.DMA((6,)),
+            pltpu.SemaphoreType.DMA((6,)),
+            pltpu.SemaphoreType.DMA((6,)),
+            pltpu.SemaphoreType.DMA((6,)),
         ],
         compiler_params=pltpu.CompilerParams(
             collective_id=0, has_side_effects=True, vmem_limit_bytes=24 * 1024 * 1024

time: 39.6 us -> 38.7 us (0.977)
  Pallas kernels: 38.1 us -> 37.2 us
    pallas_call x1, Pallas kernels: 37.3 us -> 36.4 us  [on_device(): pl.pallas_call(main_kernel, out_shape=(pltpu.VMEM((4, 4, 8, 128), f32), p...]
where the time goes in v5:
time: 38.7 us; the launch traced here: 38.5 us
  Pallas kernels  37.2 us (96%)
  between operations  1.3 us (3%)
    pallas_call x1, Pallas kernels, on_device(): pl.pallas_call(main_kernel, out_shape=(pltpu.VMEM((4, 4, 8, 128), f32), p...  36.4 us

profile of v5, /device:TPU:1, one launch (start us, length us, event | category | flops | bytes accessed | tf_op | source)
XLA Modules:
  0.0 38.5 jit_solution(9517923177643202879)
XLA Ops:
  1.3 0.0 copy-start
  1.3 36.4 %shard_map.86 = (f32[4,4,8,128]{3,2,1,0:T(8,128)S(1)}, f32[8,128]{1,0:T(8,128)S(1)}) custom-call(f32[4,4,8,128]{3,2,1,0:T(8,128)} %psi.1, f32[4,8,128]{2,1,0:T(8,128)} %pot_hbm.1, s32[1,1,1,16]{3,2,1,0:T(1,128)} %atom_hbm.1, s32[1,1,1,16,128]{4,3,2,1,0:T(8,128)} %points_hbm.1, s32[1,1,1]{2,1,0:T(1,128)S(6)} %copy.9.count, ...), custom_call_target="tpu_custom_call" | custom-call | tf_op jit(solution)/shard_map/pallas_call | solution.py:479
  37.7 0.0 copy-done
  37.7 0.8 %shard_map.87 = (f32[4,4,8,128]{3,2,1,0:T(8,128)}, f32[4,4,8,128]{3,2,1,0:T(8,128)}) custom-call(f32[4,4,8,128]{3,2,1,0:T(8,128)S(1)} %copy-done, f32[4,4,8,128]{3,2,1,0:T(8,128)S(1)} %get-tuple-element.4.image, f32[8,128]{1,0:T(8,128)S(1)} %get-tuple-element.5.gram), custom_call_target="tpu_custom_call" | custom-call | tf_op jit(solution)/shard_map/pallas_call | solution.py:519
Async XLA Ops:
  1.3 36.4 %copy-start = (f32[4,4,8,128]{3,2,1,0:T(8,128)S(1)}, f32[4,4,8,128]{3,2,1,0:T(8,128)}, u32[]{:S(2)}) copy-start(f32[4,4,8,128]{3,2,1,0:T(8,128)} %psi.1) | copy-start | bytes 196612

commit v6 on v5

--- a/solution.py
+++ b/solution.py
@@ -39,6 +39,18 @@
 
 def sublanes(shape):
     return lax.broadcasted_iota(jnp.int32, shape, len(shape) - 2)
+
+
+def pick_sum(choice, v):
+    f32, bf16 = jnp.float32, jnp.bfloat16
+    high = v.astype(bf16)
+    rest = v - high.astype(f32)
+    mid = rest.astype(bf16)
+    low = (rest - mid.astype(f32)).astype(bf16)
+    parts = jnp.dot(
+        choice.astype(bf16), jnp.concatenate([high, mid, low], axis=1), preferred_element_type=f32
+    )
+    return parts[:, 0:128] + (parts[:, 128:256] + parts[:, 256:384])
 
 
 def row_sum(v):
@@ -67,8 +79,6 @@
         pltpu.make_async_copy(coup_hbm, coup, lsem.at[4]),
         pltpu.make_async_copy(pot_hbm, pot, lsem.at[5]),
     ]
-    for load in loads:
-        load.start()
     x, y, z = here()
     column = x * 8 + y
     is_hub = column == HUB
@@ -86,6 +96,8 @@
 
     for delta in reversed(HALOS[:4]):
         greet(at_offset(delta))
+    for load in loads:
+        load.start()
     for d in (-1, 1):
         greet(hub_of(d))
 
@@ -115,14 +127,6 @@
 
     lane8, sub8 = lanes((8, 128)), sublanes((8, 128))
     loads[0].wait()
-
-    packed = jnp.zeros((8, 128), f32)
-    for n in range(4):
-        for zz in range(4):
-            g = n * 4 + zz
-            moved = pltpu.roll(psi[n, zz], (4 + 8 * g) % 128, 1)
-            packed = jnp.where(lane8 // 8 == g, moved, packed)
-    pk[...] = packed
 
     pl.semaphore_wait(barrier, jnp.where(is_hub, 4 + 2 + 2 + 31 * 4, 4 + 3))
     halo_copies = [
@@ -139,6 +143,14 @@
     ]
     for halo in halos[:4]:
         halo.start()
+
+    packed = jnp.zeros((8, 128), f32)
+    for n in range(4):
+        for zz in range(4):
+            g = n * 4 + zz
+            moved = pltpu.roll(psi[n, zz], (4 + 8 * g) % 128, 1)
+            packed = jnp.where(lane8 // 8 == g, moved, packed)
+    pk[...] = packed
 
     @pl.when(jnp.logical_not(is_hub))
     def _():
@@ -187,9 +199,7 @@
             block = jnp.where(lane_n == n, part, block)
         keep = (lane_p == sub8) & (lane_k == kind_of[b])
         blocks.append(jnp.where(keep, block, 0.0))
-    msg[...] = jnp.dot(
-        select, jnp.concatenate(blocks, axis=0), precision=HIGH, preferred_element_type=f32
-    )
+    msg[...] = pick_sum(select, jnp.concatenate(blocks, axis=0))
 
     def send_rows(d):
         src, dst = msg.at[pl.ds(16 * (d + 1), 9)], r1.at[32 * (d + 1) + column, pl.ds(0, 9)]
@@ -201,9 +211,6 @@
     @pl.when(jnp.logical_not(is_hub))
     def _():
         send_rows(0)
-
-    for halo in halos[4:]:
-        halo.start()
 
     li, si = lanes((128, 128)), sublanes((128, 128))
     away = (li - si) & 127
@@ -267,6 +274,9 @@
             row_own.at[pl.ds(0, 1)], kr.at[column, pl.ds(0, 1)], csend.at[5], crecv.at[5], hub_of(0)
         ).start()
 
+    for halo in halos[4:]:
+        halo.start()
+
     @pl.when(is_hub)
     def _():
         kr[HUB] = row_own[...]
@@ -318,14 +328,10 @@
         wait_bytes(r1.at[pl.ds(0, 95), pl.ds(0, 9)], crecv.at[0])
         gathered_rows = (r1[pl.ds(0, 32)] + r1[pl.ds(64, 32)]) + r1[pl.ds(32, 32)]
         gathered_rows = jnp.where(sublanes((32, 16, 128)) < 9, gathered_rows, 0.0)
-        coef = jnp.dot(
-            collect, gathered_rows.reshape(512, 128), precision=HIGH, preferred_element_type=f32
-        )
+        coef = pick_sum(collect, gathered_rows.reshape(512, 128))
         applied = jnp.dot(coef, couple, precision=HIGH, preferred_element_type=f32)
 
-        stage[:, pl.ds(8, 16)] = jnp.dot(
-            spread_out, applied, precision=HIGH, preferred_element_type=f32
-        ).reshape(32, 16, 128)
+        stage[:, pl.ds(8, 16)] = pick_sum(spread_out, applied).reshape(32, 16, 128)
 
         def hand_out(c, d):
             first, rows = (0, 17) if d == 0 else (8, 9)

time: 38.7 us -> 38.6 us (level)
  no operation moved by 1% of the time
where the time goes in v6:
time: 38.6 us; the launch traced here: 38.4 us
  Pallas kernels  37.1 us (96%)
  between operations  1.3 us (3%)
    pallas_call x1, Pallas kernels, on_device(): pl.pallas_call(main_kernel, out_shape=(pltpu.VMEM((4, 4, 8, 128), f32), p...  36.3 us

profile of v6, /device:TPU:1, one launch (start us, length us, event | category | flops | bytes accessed | tf_op | source)
XLA Modules:
  0.0 38.4 jit_solution(4740837228682826265)
XLA Ops:
  1.3 0.0 copy-start
  1.3 36.3 %shard_map.86 = (f32[4,4,8,128]{3,2,1,0:T(8,128)S(1)}, f32[8,128]{1,0:T(8,128)S(1)}) custom-call(f32[4,4,8,128]{3,2,1,0:T(8,128)} %psi.1, f32[4,8,128]{2,1,0:T(8,128)} %pot_hbm.1, s32[1,1,1,16]{3,2,1,0:T(1,128)} %atom_hbm.1, s32[1,1,1,16,128]{4,3,2,1,0:T(8,128)} %points_hbm.1, s32[1,1,1]{2,1,0:T(1,128)S(6)} %copy.9.count, ...), custom_call_target="tpu_custom_call" | custom-call | tf_op jit(solution)/shard_map/pallas_call | solution.py:485
  37.6 0.0 copy-done
  37.6 0.8 %shard_map.87 = (f32[4,4,8,128]{3,2,1,0:T(8,128)}, f32[4,4,8,128]{3,2,1,0:T(8,128)}) custom-call(f32[4,4,8,128]{3,2,1,0:T(8,128)S(1)} %copy-done, f32[4,4,8,128]{3,2,1,0:T(8,128)S(1)} %get-tuple-element.4.image, f32[8,128]{1,0:T(8,128)S(1)} %get-tuple-element.5.gram), custom_call_target="tpu_custom_call" | custom-call | tf_op jit(solution)/shard_map/pallas_call | solution.py:525
Async XLA Ops:
  1.3 36.4 %copy-start = (f32[4,4,8,128]{3,2,1,0:T(8,128)S(1)}, f32[4,4,8,128]{3,2,1,0:T(8,128)}, u32[]{:S(2)}) copy-start(f32[4,4,8,128]{3,2,1,0:T(8,128)} %psi.1) | copy-start | bytes 196612
